TPU v7x, 1024 devices: a whole 8x8x8 slice. The times are simulated.
1024 devices in a mesh: dp: 8 (over z), fsdp: 16 (over x, core), tensor: 8 (over y).
Axes of the slice: x: 8, y: 8, z: 8, core: 2. Of those that a mesh axis runs over, the one named last changes fastest.
Arguments:
- grad_parts: bfloat16 [8, 8, 8, 16, 5, 128, 128], P('dp', None, 'tensor', 'fsdp'), may hold values from -6 to 6
- master: float32 [8, 8, 16, 5, 128, 128], P('dp', 'tensor', 'fsdp'), may hold values from -0.12 to 0.12
- m_state: bfloat16 [8, 8, 16, 5, 128, 128], P('dp', 'tensor', 'fsdp'), may hold values from -6 to 6
- v_state: bfloat16 [8, 8, 16, 5, 128, 128], P('dp', 'tensor', 'fsdp'), may hold values from 0.5 to 8
- residual_carry: float32 [8, 8, 16, 5, 128, 128], P('dp', 'tensor', 'fsdp'), may hold values from -0.18 to 0.18
- sel_counts: int32 [8, 8, 16], P('dp', 'tensor', 'fsdp'), may hold values from 1 to 5, 32 in all within a row
- sel_order: int32 [8, 8, 16, 5], P('dp', 'tensor', 'fsdp'), may hold values from 0 to 4, each once within a row
- rollout_weight: bfloat16 [5120, 16384], P(None, ('dp', 'tensor')), may hold values from -0.078125 to 0.078125
- decode_in: bfloat16 [16, 80, 4, 5120], P('fsdp'), may hold values from -6 to 6
Outputs:
- new_master: float32 [8, 8, 16, 5, 128, 128], P('dp', 'tensor', 'fsdp')
- new_m: bfloat16 [8, 8, 16, 5, 128, 128], P('dp', 'tensor', 'fsdp')
- new_v: bfloat16 [8, 8, 16, 5, 128, 128], P('dp', 'tensor', 'fsdp')
- new_carry: float32 [8, 8, 16, 5, 128, 128], P('dp', 'tensor', 'fsdp')
- decode_out: bfloat16 [16, 80, 4, 16384], P('fsdp', None, None, ('dp', 'tensor'))
Inputs may be any that keep to these rules, and one draw needn't show every extreme that they name: `sel_counts`: among the 16 owners of one column group (fixed q and t) the counts add up to exactly 32, and some owner sends exactly 5 blocks. `sel_order`: each owner's row names each of its 5 blocks once.
All inputs are finite; a program needn't handle non-finite values.
Results may differ from a plain program's by a relative error of at most 0.012.
Values may be sent and summed in bfloat16 or wider, within the bound.
No kernel may reach another device: no remote copies, remote signals or barrier semaphores. Data moves between devices by JAX's collectives and lax.ppermute only.
A program may use at most 32 MiB of HBM per device.

v0:
```python
import jax
import jax.numpy as jnp
from jax import lax
from jax.sharding import PartitionSpec as P

adam_rate = 0.01
decay_first = 0.9
decay_second = 0.95
adam_epsilon = 1e-08
weight_decay = 0.1
adam_count = 10


def chosen_blocks(sel_counts, sel_order):
    per_owner = sel_order.shape[-1]
    block_ids = jnp.arange(per_owner, dtype=jnp.int32)
    live_slots = block_ids < sel_counts[..., None]
    matches = sel_order[..., :, None] == block_ids
    return jnp.any(matches & live_slots[..., :, None], axis=-2)


def adam_update(grad_sum, master, m_state, v_state, residual_carry):
    first = decay_first * m_state.astype(jnp.float32) + (1.0 - decay_first) * grad_sum
    second = decay_second * v_state.astype(jnp.float32) + (1.0 - decay_second) * grad_sum * grad_sum
    first_moment = first / (1.0 - decay_first**adam_count)
    second_moment = second / (1.0 - decay_second**adam_count)
    update = adam_rate * (
        first_moment / (jnp.sqrt(second_moment) + adam_epsilon) + weight_decay * master
    )
    return (
        master - update,
        first.astype(jnp.bfloat16),
        second.astype(jnp.bfloat16),
        residual_carry - update,
    )


def split_outbound(accumulated, chosen):
    outbound = jnp.where(
        chosen[..., None, None], accumulated.astype(jnp.bfloat16), jnp.zeros((), jnp.bfloat16)
    )
    return (outbound, accumulated - outbound.astype(jnp.float32))


def blocks_to_dense(blocks, row_blocks, col_blocks):
    groups = blocks.shape[0]
    tile_size = blocks.shape[-1]
    arranged = blocks.reshape(groups, row_blocks, col_blocks, tile_size, tile_size)
    arranged = arranged.transpose(1, 3, 0, 2, 4)
    return arranged.reshape(row_blocks * tile_size, groups * col_blocks * tile_size)


def on_device(
    grad_parts,
    master,
    m_state,
    v_state,
    residual_carry,
    sel_counts,
    sel_order,
    rollout_weight,
    decode_in,
):
    tile_size = grad_parts.shape[-1]
    grad_sum = (
        lax.psum_scatter(
            grad_parts.astype(jnp.float32).astype(jnp.bfloat16),
            "dp",
            scatter_dimension=1,
            tiled=True,
        )
        .astype(jnp.float32)
        .reshape(master.shape)
    )
    new_master, new_m, new_v, accumulated = adam_update(
        grad_sum, master, m_state, v_state, residual_carry
    )
    chosen = chosen_blocks(sel_counts, sel_order)
    outbound, new_carry = split_outbound(accumulated, chosen)
    gathered = lax.all_gather(outbound, "fsdp", axis=2, tiled=True)
    delta_blocks = gathered.reshape(-1, tile_size, tile_size)
    model_width = rollout_weight.shape[0]
    group_width = rollout_weight.shape[1]
    delta_dense = blocks_to_dense(
        delta_blocks[None], model_width // tile_size, group_width // tile_size
    )
    patched = (rollout_weight.astype(jnp.float32) + delta_dense.astype(jnp.float32)).astype(
        jnp.bfloat16
    )
    flat_rows = decode_in.reshape(-1, model_width)
    decode_out = jnp.dot(flat_rows, patched, preferred_element_type=jnp.float32).astype(
        jnp.bfloat16
    )
    decode_out = decode_out.reshape(
        decode_in.shape[0], decode_in.shape[1], decode_in.shape[2], group_width
    )
    return (new_master, new_m, new_v, new_carry, decode_out)


def solution(mesh):
    return jax.shard_map(
        on_device,
        mesh=mesh,
        in_specs=(
            P("dp", None, "tensor", "fsdp", None, None, None),
            P("dp", "tensor", "fsdp", None, None, None),
            P("dp", "tensor", "fsdp", None, None, None),
            P("dp", "tensor", "fsdp", None, None, None),
            P("dp", "tensor", "fsdp", None, None, None),
            P("dp", "tensor", "fsdp"),
            P("dp", "tensor", "fsdp", None),
            P(None, ("dp", "tensor")),
            P("fsdp", None, None, None),
        ),
        out_specs=(
            P("dp", "tensor", "fsdp", None, None, None),
            P("dp", "tensor", "fsdp", None, None, None),
            P("dp", "tensor", "fsdp", None, None, None),
            P("dp", "tensor", "fsdp", None, None, None),
            P("fsdp", None, None, ("dp", "tensor")),
        ),
        check_vma=False,
    )
```

profile of v0, /device:TPU:1, one launch (start us, length us, event | category | flops | bytes accessed | tf_op | source)
XLA Modules:
  0.0 134.1 jit_solution(14364901891894542918)
XLA Ops:
  7.2 0.0 reduce-scatter.2.cloned.1.call-start
  7.2 0.7 reduce-scatter.2.cloned.1.call-update
  7.9 0.0 all-gather.2.cloned.1.call-start
  8.6 0.7 fusion.19
  9.3 56.4 %reduce-scatter.2.cloned.1.call-done = bf16[1,1,1,1,5,128,128]{6,5,4,3,2,1,0:T(8,128)(2,1)} async-done(((bf16[1,8,1,1,5,128,128]{6,5,4,3,2,1,0:T(8,128)(2,1)}), bf16[1,1,1,1,5,128,128]{6,5,4,3,2,1,0:T(8,128)(2,1)}) %reduce-scatter.2.cloned.1.call-update) | async-done | bytes 163856 | tf_op jit(solution)/shard_map/reduce_scatter | solution.py:66
  65.8 2.3 %convert_select_fusion = (bf16[1,1,1,5,128,128]{5,4,3,1,0,2:T(8,128)(2,1)}, f32[1,1,1,5,128,128]{5,4,3,1,0,2:T(8,128)}) fusion(pred[5]{0:T(512)(128)(4,1)S(1)} %fusion.19, f32[1,1,1,5,128,128]{5,4,3,2,1,0:T(8,128)} %param.13, f32[1,1,1,5,128,128]{5,4,3,2,1,0:T(8,128)} %param.10, bf16[1,1,1,5,128,128]{5,4,3,2,1,0:T(8,128)(2,1)} %param.12, ...), kind=kLoop, calls=%fused_computation.22 | loop fusion | flops 1638400 | bytes 1638405 | tf_op jit(solution)/shard_map/jit(_where)/select_n | solution.py:39
  68.1 0.0 all-gather.2.cloned.1.call-update
  68.1 0.0 copy-start
  68.1 4.6 %reshape.143 = bf16[320,5120]{1,0:T(8,128)(2,1)S(1)} reshape(bf16[1,80,4,5120]{3,2,1,0:T(4,128)(2,1)} %param.17) | data formatting | bytes 6553600 | tf_op jit(solution)/shard_map/reshape | solution.py:90
  72.7 0.0 copy-done
  72.7 2.3 %subtract_bitcast_fusion = (f32[1,1,1,5,128,128]{5,4,3,2,1,0:T(8,128)}, f32[1,1,1,5,128,128]{5,4,3,2,1,0:T(8,128)}, bf16[1,1,1,5,128,128]{5,4,3,2,1,0:T(8,128)(2,1)}, bf16[1,1,1,5,128,128]{5,4,3,2,1,0:T(8,128)(2,1)}) fusion(f32[1,1,1,5,128,128]{5,4,3,1,0,2:T(8,128)} %get-tuple-element.16, f32[1,1,1,5,128,128]{5,4,3,2,1,0:T(8,128)} %param.13, ...), kind=kLoop, calls=%fused_computation.17 | loop fusion | flops 1474560 | bytes 2457605
  75.1 41.8 %all-gather.2.cloned.1.call-done = bf16[1,1,16,5,128,128]{5,4,3,1,0,2:T(8,128)(2,1)} async-done(((bf16[1,1,1,5,128,128]{5,4,3,1,0,2:T(8,128)(2,1)}), bf16[1,1,16,5,128,128]{5,4,3,1,0,2:T(8,128)(2,1)}) %all-gather.2.cloned.1.call-update) | async-done | bytes 2621456 | tf_op jit(solution)/shard_map/all_gather | solution.py:80
  116.8 2.4 %convert_bitcast_fusion = f32[40,128,1,2,128]{4,1,3,0,2:T(8,128)S(1)} fusion(bf16[1,40,2,128,128]{4,3,2,1,0:T(8,128)(2,1)} %bitcast.64), kind=kLoop, calls=%fused_computation.2 | loop fusion | flops 1310720 | bytes 7864320 | tf_op jit(solution)/shard_map/convert_element_type | solution.py:87
  119.3 4.4 %copy.30 = f32[40,128,1,2,128]{4,3,1,0,2:T(2,128)S(1)} copy(f32[40,128,1,2,128]{4,1,3,0,2:T(8,128)S(1)} %convert_bitcast_fusion) | data formatting | bytes 10485760 | tf_op jit(solution)/shard_map/convert_element_type | solution.py:87
  123.7 2.9 %fusion.6 = bf16[320,256]{1,0:T(8,128)(2,1)S(1)} fusion(bf16[320,5120]{1,0:T(8,128)(2,1)S(1)} %reshape.143, f32[640,8,2,128]{3,2,1,0:T(2,128)S(1)} %bitcast.63, bf16[5120,256]{1,0:T(8,128)(2,1)} %param.16), kind=kOutput, calls=%fused_computation.5 | convolution fusion | flops 842874880 | bytes 11304960 | tf_op jit(solution)/shard_map/dot_general | solution.py:91
  126.6 0.7 reshape.144
  (1 shorter events, 0.0 us)
Async XLA Ops:
  7.2 58.6 %reduce-scatter.2.cloned.1.call-start = ((), (), s32[]{:S(2)}) async-start(), calls=%async_computation.1 | async-start | bytes 1474560 | tf_op jit(solution)/shard_map/reduce_scatter | solution.py:66
  7.9 108.9 %all-gather.2.cloned.1.call-start = ((), (), s32[]{:S(2)}) async-start(), calls=%async_computation.2 | async-start | bytes 2785280 | tf_op jit(solution)/shard_map/all_gather | solution.py:80
  68.1 4.6 %copy-start = (bf16[1,1,1,5,128,128]{5,4,3,2,1,0:T(8,128)(2,1)S(1)}, bf16[1,1,1,5,128,128]{5,4,3,2,1,0:T(8,128)(2,1)}, u32[]{:S(2)}) copy-start(bf16[1,1,1,5,128,128]{5,4,3,2,1,0:T(8,128)(2,1)} %param.12) | copy-start | bytes 491524
Sparse Core Ops, SparseCore 0:
  11.4 54.3 reduce-scatter.1
  69.1 47.7 all-gather.1
where the time goes:
time: 134 us
  waiting for transfers between devices  98.9 us (74%)
  between operations  14.7 us (11%)
  local copies, waits for them, and re-layouts  9.75 us (7%)
  other arithmetic  7.81 us (6%)
  matrix products  2.88 us (2%)
    reduce_scatter x1, waiting for transfers between devices, on_device(): lax.psum_scatter(grad_parts.astype(jnp.float32).astype(jnp.bfloat16), 'dp...  56.4 us
    all_gather x1, waiting for transfers between devices, on_device(): gathered = lax.all_gather(outbound, 'fsdp', axis=2, tiled=True)  41.8 us
    reshape x1, local copies, waits for them, and re-layouts, on_device(): flat_rows = decode_in.reshape(-1, model_width)  4.59 us
    convert_element_type x1, local copies, waits for them, and re-layouts, on_device(): delta_dense.astype(jnp.float32)  4.44 us
    dot_general x1, matrix products, on_device(): jnp.dot(flat_rows, patched, preferred_element_type=jnp.float32)  2.88 us
  transfers between devices with their start and end apart: 2, of which 2 were waited for; matrix products, arithmetic and copies ran while one was open for 6% of the time, Pallas kernels for 0%

commit v1 on v0

--- a/solution.py
+++ b/solution.py
@@ -1,6 +1,8 @@
 import jax
 import jax.numpy as jnp
 from jax import lax
+from jax.experimental import pallas as pl
+from jax.experimental.pallas import tpu as pltpu
 from jax.sharding import PartitionSpec as P
 
 adam_rate = 0.01
@@ -42,12 +44,54 @@
     return (outbound, accumulated - outbound.astype(jnp.float32))
 
 
-def blocks_to_dense(blocks, row_blocks, col_blocks):
-    groups = blocks.shape[0]
-    tile_size = blocks.shape[-1]
-    arranged = blocks.reshape(groups, row_blocks, col_blocks, tile_size, tile_size)
-    arranged = arranged.transpose(1, 3, 0, 2, 4)
-    return arranged.reshape(row_blocks * tile_size, groups * col_blocks * tile_size)
+wire_scale = 256.0
+
+
+def shifted(size, step):
+    return [(i, (i + step) % size) for i in range(size)]
+
+
+def sum_at_owner(parts):
+    size = parts.shape[0]
+    here = lax.axis_index("dp")
+    even = here % 2 == 0
+
+    def part(places):
+        return lax.dynamic_index_in_dim(parts, (here + places) % size, 0, keepdims=False)
+
+    def wide(x):
+        return x.astype(jnp.float32)
+
+    opposite = [(i, (i + 2) % size if i % 2 == 0 else (i - 2) % size) for i in range(size)]
+    up = lax.ppermute(jnp.stack([part(3), part(1)]), "dp", shifted(size, 1))
+    down = lax.ppermute(jnp.stack([part(-3), part(-1)]), "dp", shifted(size, -1))
+    far = wide(lax.ppermute(part(4), "dp", opposite))
+    up_two = wide(part(2)) + wide(up[0]) + jnp.where(even, far, 0.0)
+    down_two = wide(part(-2)) + wide(down[0]) + jnp.where(even, 0.0, far)
+    up_two = lax.ppermute(up_two.astype(parts.dtype), "dp", shifted(size, 2))
+    down_two = lax.ppermute(down_two.astype(parts.dtype), "dp", shifted(size, -2))
+    return wide(part(0)) + wide(up[1]) + wide(down[1]) + wide(up_two) + wide(down_two)
+
+
+def add_delta_product(rows_ref, blocks_ref, base_ref, out_ref):
+    tile = blocks_ref.shape[-1]
+    across = base_ref.shape[1] // tile
+    deep = 5
+    total = base_ref[...]
+    for first in range(0, rows_ref.shape[1] // tile, deep):
+        weights = jnp.concatenate(
+            [
+                jnp.concatenate([blocks_ref[r * across + c] for c in range(across)], axis=1)
+                for r in range(first, first + deep)
+            ],
+            axis=0,
+        )
+        total += jnp.dot(
+            rows_ref[:, first * tile : (first + deep) * tile],
+            weights,
+            preferred_element_type=jnp.float32,
+        )
+    out_ref[...] = total.astype(out_ref.dtype)
 
 
 def on_device(
@@ -62,38 +106,28 @@
     decode_in,
 ):
     tile_size = grad_parts.shape[-1]
-    grad_sum = (
-        lax.psum_scatter(
-            grad_parts.astype(jnp.float32).astype(jnp.bfloat16),
-            "dp",
-            scatter_dimension=1,
-            tiled=True,
-        )
-        .astype(jnp.float32)
-        .reshape(master.shape)
-    )
+    parts = grad_parts.reshape(grad_parts.shape[1], -1, tile_size, tile_size)
+    grad_sum = sum_at_owner(parts).reshape(master.shape)
     new_master, new_m, new_v, accumulated = adam_update(
         grad_sum, master, m_state, v_state, residual_carry
     )
     chosen = chosen_blocks(sel_counts, sel_order)
     outbound, new_carry = split_outbound(accumulated, chosen)
-    gathered = lax.all_gather(outbound, "fsdp", axis=2, tiled=True)
-    delta_blocks = gathered.reshape(-1, tile_size, tile_size)
-    model_width = rollout_weight.shape[0]
-    group_width = rollout_weight.shape[1]
-    delta_dense = blocks_to_dense(
-        delta_blocks[None], model_width // tile_size, group_width // tile_size
-    )
-    patched = (rollout_weight.astype(jnp.float32) + delta_dense.astype(jnp.float32)).astype(
-        jnp.bfloat16
-    )
+    model_width, group_width = rollout_weight.shape
     flat_rows = decode_in.reshape(-1, model_width)
-    decode_out = jnp.dot(flat_rows, patched, preferred_element_type=jnp.float32).astype(
-        jnp.bfloat16
-    )
-    decode_out = decode_out.reshape(
-        decode_in.shape[0], decode_in.shape[1], decode_in.shape[2], group_width
-    )
+    base = jnp.dot(flat_rows, rollout_weight, preferred_element_type=jnp.float32)
+    sent = (outbound.astype(jnp.float32) * wire_scale).astype(jnp.float16)
+    gathered = lax.all_gather(sent.reshape(-1, tile_size, tile_size), "fsdp", axis=0, tiled=True)
+    delta_blocks = (gathered.astype(jnp.float32) * (1.0 / wire_scale)).astype(jnp.bfloat16)
+    decode_out = pl.pallas_call(
+        add_delta_product,
+        out_shape=jax.ShapeDtypeStruct(base.shape, jnp.bfloat16),
+        in_specs=[pl.BlockSpec(memory_space=pltpu.VMEM)] * 3,
+        out_specs=pl.BlockSpec(memory_space=pltpu.VMEM),
+        compiler_params=pltpu.CompilerParams(vmem_limit_bytes=32 * 1024 * 1024),
+        name="add_delta_product",
+    )(flat_rows, delta_blocks, base)
+    decode_out = decode_out.reshape(decode_in.shape[:3] + (group_width,))
     return (new_master, new_m, new_v, new_carry, decode_out)
 
 

time: 134 us -> 92 us (0.69)
  waiting for transfers between devices: 98.9 us -> 3.97 us
  blocking collectives: 0 us -> 32 us
  starting transfers between devices: 0.08 us -> 29.1 us
  between operations: 14.7 us -> 1.53 us
  other arithmetic: 7.81 us -> 10.9 us
    reduce_scatter x1 -> x0, waiting for transfers between devices: 56.4 us -> none  [on_device(): lax.psum_scatter(grad_parts.astype(jnp.float32).astype(jnp.bfloat16), 'dp...]
    all_gather x1 -> x0, waiting for transfers between devices: 41.8 us -> none  [on_device(): gathered = lax.all_gather(outbound, 'fsdp', axis=2, tiled=True)]
    all_gather x0 -> x1, blocking collectives: none -> 32 us  [on_device(): lax.all_gather(sent.reshape(-1, tile_size, tile_size), 'fsdp', axis=0, ti...]
    ppermute x0 -> x5, starting transfers between devices: none -> 29.1 us  [the longest x1 17.9 us: sum_at_owner(): lax.ppermute(jnp.stack([part(-3), part(-1)]), 'dp', shifted(size, -1))]
    convert_element_type x1 -> x4, other arithmetic: 2.42 us -> 7.12 us  [the longest x1 2.57 us: on_device(): sent = (outbound.astype(jnp.float32) * wire_scale).astype(jnp.float16)]
    convert_element_type x1 -> x0, local copies, waits for them, and re-layouts: 4.44 us -> none  [on_device(): delta_dense.astype(jnp.float32)]
    ppermute x0 -> x5, waiting for transfers between devices: none -> 3.97 us  [the longest x1 3.39 us: sum_at_owner(): up_two = lax.ppermute(up_two.astype(parts.dtype), 'dp', shifted(size, 2))]
    select_n x1 -> x0, other arithmetic: 2.32 us -> none  [split_outbound(): jnp.where(chosen[..., None, None], accumulated.astype(jnp.bfloat16), jnp....]
  transfers between devices with their start and end apart: 2 -> 5, of which waited for: 2 -> 2; matrix products, arithmetic and copies ran while one was open for 6% -> 11% of each run, Pallas kernels for 0% -> 0%
where the time goes in v1:
time: 92 us; the launch traced here: 91.5 us
  blocking collectives  32 us (35%)
  starting transfers between devices  29.1 us (32%)
  other arithmetic  10.9 us (12%)
  local copies, waits for them, and re-layouts  9.97 us (11%)
  waiting for transfers between devices  3.97 us (4%)
  matrix products  2.97 us (3%)
  between operations  1.53 us (2%)
  Pallas kernels  1.16 us (1%)
    all_gather x1, blocking collectives, on_device(): lax.all_gather(sent.reshape(-1, tile_size, tile_size), 'fsdp', axis=0, ti...  32 us
    ppermute x1, starting transfers between devices, sum_at_owner(): lax.ppermute(jnp.stack([part(-3), part(-1)]), 'dp', shifted(size, -1))  17.9 us
    reshape x1, local copies, waits for them, and re-layouts, on_device(): flat_rows = decode_in.reshape(-1, model_width)  5.96 us
    ppermute x1, starting transfers between devices, sum_at_owner(): lax.ppermute(down_two.astype(parts.dtype), 'dp', shifted(size, -2))  4.35 us
    ppermute x1, waiting for transfers between devices, sum_at_owner(): up_two = lax.ppermute(up_two.astype(parts.dtype), 'dp', shifted(size, 2))  3.39 us
    ppermute x1, starting transfers between devices, sum_at_owner(): up_two = lax.ppermute(up_two.astype(parts.dtype), 'dp', shifted(size, 2))  3.04 us
    dot_general x1, matrix products, on_device(): jnp.dot(flat_rows, rollout_weight, preferred_element_type=jnp.float32)  2.97 us
    convert_element_type x1, other arithmetic, on_device(): sent = (outbound.astype(jnp.float32) * wire_scale).astype(jnp.float16)  2.57 us
  transfers between devices with their start and end apart: 5, of which 2 were waited for; matrix products, arithmetic and copies ran while one was open for 11% of the time, Pallas kernels for 0%

profile of v1, /device:TPU:1, one launch (start us, length us, event | category | flops | bytes accessed | tf_op | source)
XLA Modules:
  0.0 91.5 jit_solution(11216592360058840728)
XLA Ops:
  0.6 0.0 copy-start
  0.7 2.1 %dynamic-slice_bitcast_fusion.4 = (bf16[1,5,128,128]{3,2,1,0:T(8,128)(2,1)S(1)}, bf16[1,5,128,128]{3,2,1,0:T(8,128)(2,1)S(1)}, bf16[1,5,128,128]{3,2,1,0:T(8,128...) fusion(bf16[1,8,1,1,5,128,128]{6,5,4,3,2,1,0:T(8,128)(2,1)} %param.9, s32[]{:T(128)S(6)} %select_n.85, ...), kind=kLoop, calls=%fused_computation.43 | loop fusion | bytes 1638420 | tf_op jit(solution)/shard_map/jit(dynamic_index_in_dim)/dynamic_slice | solution.py:60
  2.9 0.8 pad_maximum_fusion.1
  3.6 17.9 %collective-permute-start.1 = (bf16[2,5,128,128]{3,2,1,0:T(8,128)(2,1)}, bf16[2,5,128,128]{3,2,1,0:T(8,128)(2,1)S(1)}, u32[]{:S(2)}, u32[]{:S(2)}) collective-permute-start(bf16[2,5,128,128]{3,2,1,0:T(8,128)(2,1)} %pad_maximum_fusion.1), channel_id=1, source_target_pairs={{0,896},{128,0},{256,128},{384,256},{512,384},{640,512},{768,640},... | collective-permute-start | bytes 983048 | tf_op jit(solution)/shard_map/ppermute | solution.py:67
  21.5 0.8 pad_maximum_fusion
  22.2 1.9 %collective-permute-start = (bf16[2,5,128,128]{3,2,1,0:T(8,128)(2,1)}, bf16[2,5,128,128]{3,2,1,0:T(8,128)(2,1)}, u32[]{:S(2)}, u32[]{:S(2)}) collective-permute-start(bf16[2,5,128,128]{3,2,1,0:T(8,128)(2,1)} %pad_maximum_fusion), channel_id=1, source_target_pairs={{0,128},{128,256},{256,384},{384,512},{512,640},{640,768},{768,896... | collective-permute-start | bytes 983048 | tf_op jit(solution)/shard_map/ppermute | solution.py:66
  24.2 1.9 %collective-permute-start.2 = (bf16[5,128,128]{2,1,0:T(8,128)(2,1)}, bf16[5,128,128]{2,1,0:T(8,128)(2,1)}, u32[]{:S(2)}, u32[]{:S(2)}) collective-permute-start(bf16[5,128,128]{2,1,0:T(8,128)(2,1)} %get-tuple-element.24), channel_id=1, source_target_pairs={{0,256},{128,896},{256,512},{384,128},{512,768},{640,384},{768,0},... | collective-permute-start | bytes 491528 | tf_op jit(solution)/shard_map/ppermute | solution.py:68
  26.1 6.0 %reshape.128.rows_ref = bf16[320,5120]{1,0:T(8,128)(2,1)} reshape(bf16[1,80,4,5120]{3,2,1,0:T(4,128)(2,1)} %param.17) | data formatting | bytes 6553600 | tf_op jit(solution)/shard_map/reshape | solution.py:117
  32.0 0.0 copy-done
  32.0 0.0 copy-start.4
  32.1 0.0 copy-start.2
  32.1 3.0 %fusion.21.base_ref = f32[320,256]{1,0:T(8,128)S(1)} fusion(bf16[320,5120]{1,0:T(8,128)(2,1)} %reshape.128.rows_ref, bf16[5120,256]{1,0:T(8,128)(2,1)S(1)} %copy-done), kind=kOutput, calls=%fused_computation.48 | convolution fusion | flops 838860800 | bytes 6225920 | tf_op jit(solution)/shard_map/dot_general | solution.py:118
  35.7 0.6 collective-permute-done.2
  36.3 0.0 collective-permute-done.1
  36.3 0.0 copy-start.3
  36.3 0.0 collective-permute-done
  36.3 2.1 %fusion.2 = (bf16[5,128,128]{2,1,0:T(8,128)(2,1)}, bf16[5,128,128]{2,1,0:T(8,128)(2,1)}) fusion(bf16[5,128,128]{2,1,0:T(8,128)(2,1)} %collective-permute-done.2, bf16[2,5,128,128]{3,2,1,0:T(8,128)(2,1)} %collective-permute-done, bf16[1,8,1,1,5,128,128]{6,5,4,3,2,1,0:T(8,128)(2,1)} %param.9, s32[]{:T(128)S(6)} %select_n.93, pred[]{:T(512)S(6)} %eq.34, ...), kind=kLoop, calls=%fused_computation.8 | loop fusion | flops 1064960 | bytes 1146889 | tf_op jit(solution)/shard_map/convert_element_type | solution.py:71
  38.4 3.0 %collective-permute-start.3 = (bf16[5,128,128]{2,1,0:T(8,128)(2,1)}, bf16[5,128,128]{2,1,0:T(8,128)(2,1)}, u32[]{:S(2)}, u32[]{:S(2)}) collective-permute-start(bf16[5,128,128]{2,1,0:T(8,128)(2,1)} %get-tuple-element.18), channel_id=1, source_target_pairs={{0,256},{128,384},{256,512},{384,640},{512,768},{640,896},{768,0},... | collective-permute-start | bytes 491528 | tf_op jit(solution)/shard_map/ppermute | solution.py:71
  41.5 4.3 %collective-permute-start.4 = (bf16[5,128,128]{2,1,0:T(8,128)(2,1)}, bf16[5,128,128]{2,1,0:T(8,128)(2,1)}, u32[]{:S(2)}, u32[]{:S(2)}) collective-permute-start(bf16[5,128,128]{2,1,0:T(8,128)(2,1)} %get-tuple-element.19), channel_id=1, source_target_pairs={{0,768},{128,896},{256,0},{384,128},{512,256},{640,384},{768,512},... | collective-permute-start | bytes 491528 | tf_op jit(solution)/shard_map/ppermute | solution.py:72
  45.9 0.0 copy-done.4
  45.9 0.1 fusion.18
  46.0 3.4 %collective-permute-done.3 = bf16[5,128,128]{2,1,0:T(8,128)(2,1)} collective-permute-done((bf16[5,128,128]{2,1,0:T(8,128)(2,1)}, bf16[5,128,128]{2,1,0:T(8,128)(2,1)}, u32[]{:S(2)}, u32[]{:S(2)}) %collective-permute-start.3) | collective-permute-done | bytes 163872 | tf_op jit(solution)/shard_map/ppermute | solution.py:71
  49.4 0.0 copy-done.3
  49.4 0.0 collective-permute-done.4
  49.4 0.0 copy-done.2
  49.4 2.6 %fusion.6 = (f16[1,1,1,5,128,128]{5,4,2,1,0,3:T(8,128)(2,1)S(1)}, f32[1,1,1,5,128,128]{5,4,2,1,0,3:T(8,128)}, f32[5,128,128]{2,1,0:T(8,128)S(1)}) fusion(pred[5]{0:T(512)(128)(4,1)S(1)} %fusion.18, f32[1,1,1,5,128,128]{5,4,3,2,1,0:T(8,128)} %param.13, f32[1,1,1,5,128,128]{5,4,3,2,1,0:T(8,128)} %param.10, bf16[1,1,1,5,128,128]{5,4,3,2,1,0:T(8,128)(2,1)S(1)} %copy-done.2, ...), kind=kLoop, calls=%fused_computation.12 | loop fusion | flops 2539520 | bytes 2621449 | tf_op jit(solution)/shard_map/convert_element_type | solution.py:119
  51.9 32.0 %all-gather.2 = f16[1,1,1,80,128,128]{5,4,2,1,0,3:T(8,128)(2,1)S(1)} all-gather(f16[1,1,1,5,128,128]{5,4,2,1,0,3:T(8,128)(2,1)S(1)} %get-tuple-element.15), channel_id=2, replica_groups=mesh['dp'=8,'fsdp'=16,'tensor'=8] {'fsdp'}, dimensions={3}, use_global_device_ids=true | all-gather | bytes 2785280 | tf_op jit(solution)/shard_map/all_gather | solution.py:120
  84.0 0.0 copy-start.1
  84.0 0.8 fusion.blocks_ref
  84.7 1.1 %copy-done.1 = bf16[320,5120]{1,0:T(8,128)(2,1)S(1)} copy-done((bf16[320,5120]{1,0:T(8,128)(2,1)S(1)}, bf16[320,5120]{1,0:T(8,128)(2,1)}, u32[]{:S(2)}) %copy-start.1) | copy-done | bytes 3276824
  85.9 1.2 %add_delta_product.1 = bf16[320,256]{1,0:T(8,128)(2,1)S(1)} custom-call(bf16[320,5120]{1,0:T(8,128)(2,1)S(1)} %copy-done.1, bf16[80,128,128]{2,1,0:T(8,128)(2,1)S(1)} %fusion.blocks_ref, f32[320,256]{1,0:T(8,128)S(1)} %fusion.21.base_ref), custom_call_target="tpu_custom_call" | custom-call | tf_op jit(solution)/shard_map/add_delta_product/pallas_call | solution.py:122
  87.1 0.7 reshape.130
  87.8 1.6 %fusion.14 = bf16[1,1,1,5,128,128]{5,4,3,2,1,0:T(8,128)(2,1)} fusion(f32[5,128,128]{2,1,0:T(8,128)S(1)} %get-tuple-element.17, bf16[1,1,1,5,128,128]{5,4,3,2,1,0:T(8,128)(2,1)} %param.11), kind=kLoop, calls=%fused_computation.31 | loop fusion | flops 409600 | bytes 655360 | tf_op jit(solution)/shard_map/convert_element_type | solution.py:34
  89.4 2.1 %fusion.5 = (f32[1,1,1,5,128,128]{5,4,3,2,1,0:T(8,128)}, f32[1,1,1,5,128,128]{5,4,3,2,1,0:T(8,128)}, bf16[1,1,1,5,128,128]{5,4,3,2,1,0:T(8,128)(2,1)}) fusion(pred[5]{0:T(512)(128)(4,1)S(1)} %fusion.18, f32[1,1,1,5,128,128]{5,4,2,1,0,3:T(8,128)} %get-tuple-element.16, f32[1,1,1,5,128,128]{5,4,3,2,1,0:T(8,128)} %param.13, ...), kind=kLoop, calls=%fused_computation.11 | loop fusion | flops 983040 | bytes 2293765
  (1 shorter events, 0.0 us)
Async XLA Ops:
  0.6 31.4 %copy-start = (bf16[5120,256]{1,0:T(8,128)(2,1)S(1)}, bf16[5120,256]{1,0:T(8,128)(2,1)}, u32[]{:S(2)}) copy-start(bf16[5120,256]{1,0:T(8,128)(2,1)} %param.16) | copy-start | bytes 7864324
  3.6 32.7 %collective-permute-start.1 = (bf16[2,5,128,128]{3,2,1,0:T(8,128)(2,1)}, bf16[2,5,128,128]{3,2,1,0:T(8,128)(2,1)S(1)}, u32[]{:S(2)}, u32[]{:S(2)}) collective-permute-start(bf16[2,5,128,128]{3,2,1,0:T(8,128)(2,1)} %pad_maximum_fusion.1), channel_id=1, source_target_pairs={{0,896},{128,0},{256,128},{384,256},{512,384},{640,512},{768,640},... | collective-permute-start | bytes 983048 | tf_op jit(solution)/shard_map/ppermute | solution.py:67
  22.2 14.1 %collective-permute-start = (bf16[2,5,128,128]{3,2,1,0:T(8,128)(2,1)}, bf16[2,5,128,128]{3,2,1,0:T(8,128)(2,1)}, u32[]{:S(2)}, u32[]{:S(2)}) collective-permute-start(bf16[2,5,128,128]{3,2,1,0:T(8,128)(2,1)} %pad_maximum_fusion), channel_id=1, source_target_pairs={{0,128},{128,256},{256,384},{384,512},{512,640},{640,768},{768,896... | collective-permute-start | bytes 983048 | tf_op jit(solution)/shard_map/ppermute | solution.py:66
  24.2 12.1 %collective-permute-start.2 = (bf16[5,128,128]{2,1,0:T(8,128)(2,1)}, bf16[5,128,128]{2,1,0:T(8,128)(2,1)}, u32[]{:S(2)}, u32[]{:S(2)}) collective-permute-start(bf16[5,128,128]{2,1,0:T(8,128)(2,1)} %get-tuple-element.24), channel_id=1, source_target_pairs={{0,256},{128,896},{256,512},{384,128},{512,768},{640,384},{768,0},... | collective-permute-start | bytes 491528 | tf_op jit(solution)/shard_map/ppermute | solution.py:68
  32.0 13.8 %copy-start.4 = (s32[1,1,1,5]{3,2,1,0:T(1,128)S(1)}, s32[1,1,1,5]{3,2,1,0:T(1,128)}, u32[]{:S(2)}) copy-start(s32[1,1,1,5]{3,2,1,0:T(1,128)} %param.15) | copy-start | bytes 64
  32.1 17.3 %copy-start.2 = (bf16[1,1,1,5,128,128]{5,4,3,2,1,0:T(8,128)(2,1)S(1)}, bf16[1,1,1,5,128,128]{5,4,3,2,1,0:T(8,128)(2,1)}, u32[]{:S(2)}) copy-start(bf16[1,1,1,5,128,128]{5,4,3,2,1,0:T(8,128)(2,1)} %param.12) | copy-start | bytes 491524
  36.3 13.1 %copy-start.3 = (bf16[2,5,128,128]{3,2,1,0:T(8,128)(2,1)}, bf16[2,5,128,128]{3,2,1,0:T(8,128)(2,1)S(1)}, u32[]{:S(2)}) copy-start(bf16[2,5,128,128]{3,2,1,0:T(8,128)(2,1)S(1)} %collective-permute-done.1) | copy-start | bytes 983044
  38.4 10.9 %collective-permute-start.3 = (bf16[5,128,128]{2,1,0:T(8,128)(2,1)}, bf16[5,128,128]{2,1,0:T(8,128)(2,1)}, u32[]{:S(2)}, u32[]{:S(2)}) collective-permute-start(bf16[5,128,128]{2,1,0:T(8,128)(2,1)} %get-tuple-element.18), channel_id=1, source_target_pairs={{0,256},{128,384},{256,512},{384,640},{512,768},{640,896},{768,0},... | collective-permute-start | bytes 491528 | tf_op jit(solution)/shard_map/ppermute | solution.py:71
  41.5 7.9 %collective-permute-start.4 = (bf16[5,128,128]{2,1,0:T(8,128)(2,1)}, bf16[5,128,128]{2,1,0:T(8,128)(2,1)}, u32[]{:S(2)}, u32[]{:S(2)}) collective-permute-start(bf16[5,128,128]{2,1,0:T(8,128)(2,1)} %get-tuple-element.19), channel_id=1, source_target_pairs={{0,768},{128,896},{256,0},{384,128},{512,256},{640,384},{768,512},... | collective-permute-start | bytes 491528 | tf_op jit(solution)/shard_map/ppermute | solution.py:72
  84.0 1.9 %copy-start.1 = (bf16[320,5120]{1,0:T(8,128)(2,1)S(1)}, bf16[320,5120]{1,0:T(8,128)(2,1)}, u32[]{:S(2)}) copy-start(bf16[320,5120]{1,0:T(8,128)(2,1)} %reshape.128.rows_ref) | copy-start | bytes 9830404

commit v2 on v1

v2 whole, which is shorter than its diff:
```python
import functools

import jax
import jax.numpy as jnp
from jax import lax
from jax.experimental import pallas as pl
from jax.experimental.pallas import tpu as pltpu
from jax.sharding import PartitionSpec as P

adam_rate = 0.01
decay_first = 0.9
decay_second = 0.95
adam_epsilon = 1e-08
weight_decay = 0.1
adam_count = 10
wire_scale = 256.0

ANY = pl.BlockSpec(memory_space=pl.ANY)
VMEM = pl.BlockSpec(memory_space=pltpu.VMEM)
SMEM = pl.BlockSpec(memory_space=pltpu.SMEM)


def shifted(size, step):
    return [(i, (i + step) % size) for i in range(size)]


def wide(x):
    return x.astype(jnp.float32)


def fetch(pairs, sems):
    copies = [pltpu.make_async_copy(src, dst, sems.at[i]) for i, (src, dst) in enumerate(pairs)]
    for copy in copies:
        copy.start()
    return copies


def pack_first_round(here_ref, parts_ref, far_ref, up_ref, down_ref, sems):
    size = parts_ref.shape[0]
    here = here_ref[0]

    def part(places):
        return parts_ref.at[lax.rem(here + places, size)]

    copies = fetch(
        [
            (part(3), up_ref.at[0]),
            (part(1), up_ref.at[1]),
            (part(size - 3), down_ref.at[0]),
            (part(size - 1), down_ref.at[1]),
            (part(4), far_ref),
        ],
        sems,
    )
    for copy in copies:
        copy.wait()


def pack_second_round(
    here_ref, parts_ref, up_ref, down_ref, far_ref, up_two_ref, down_two_ref, got, sems
):
    size = parts_ref.shape[0]
    here = here_ref[0]
    copies = fetch(
        [
            (parts_ref.at[lax.rem(here + 2, size)], got.at[0]),
            (parts_ref.at[lax.rem(here + size - 2, size)], got.at[1]),
            (up_ref.at[0], got.at[2]),
            (down_ref.at[0], got.at[3]),
            (far_ref, got.at[4]),
        ],
        sems,
    )
    for copy in copies:
        copy.wait()
    far = wide(got[4])
    upward = lax.rem(here, 2) == 0
    up_two_ref[...] = (
        wide(got[0]) + wide(got[2]) + jnp.where(upward, far, jnp.zeros_like(far))
    ).astype(up_two_ref.dtype)
    down_two_ref[...] = (
        wide(got[1]) + wide(got[3]) + jnp.where(upward, jnp.zeros_like(far), far)
    ).astype(down_two_ref.dtype)


def sum_near(here_ref, parts_ref, up_ref, down_ref, near_ref, got, sems):
    copies = fetch(
        [
            (parts_ref.at[here_ref[0]], got.at[0]),
            (up_ref.at[1], got.at[1]),
            (down_ref.at[1], got.at[2]),
        ],
        sems,
    )
    for copy in copies:
        copy.wait()
    near_ref[...] = wide(got[0]) + wide(got[1]) + wide(got[2])


def adam_and_select(
    counts_ref,
    order_ref,
    near_ref,
    up_two_ref,
    down_two_ref,
    master_ref,
    m_ref,
    v_ref,
    residual_ref,
    new_master_out,
    new_m_out,
    new_v_out,
    new_carry_out,
    sent_ref,
    new_master_ref,
    new_m_ref,
    new_v_ref,
    new_carry_ref,
    sems,
):
    first_scale = adam_rate / (1.0 - decay_first**adam_count)
    second_scale = 1.0 / (1.0 - decay_second**adam_count)
    copies = []
    for b in range(near_ref.shape[0]):
        grad_sum = near_ref[b] + wide(up_two_ref[b]) + wide(down_two_ref[b])
        master = master_ref[b]
        first = decay_first * wide(m_ref[b]) + (1.0 - decay_first) * grad_sum
        second = decay_second * wide(v_ref[b]) + (1.0 - decay_second) * grad_sum * grad_sum
        update = (first * first_scale) / (
            jnp.sqrt(second * second_scale) + adam_epsilon
        ) + (adam_rate * weight_decay) * master
        accumulated = residual_ref[b] - update
        chosen = functools.reduce(
            jnp.logical_or,
            [
                jnp.logical_and(s < counts_ref[0], order_ref[s] == b)
                for s in range(order_ref.shape[0])
            ],
        )
        outbound = accumulated.astype(sent_ref.dtype)
        outbound = jnp.where(chosen, wide(outbound), jnp.zeros_like(accumulated))
        sent_ref[b] = outbound.astype(sent_ref.dtype)
        new_carry_ref[b] = accumulated - outbound
        new_master_ref[b] = master - update
        new_m_ref[b] = first.astype(new_m_ref.dtype)
        new_v_ref[b] = second.astype(new_v_ref.dtype)
        copies += fetch(
            [
                (new_master_ref.at[b], new_master_out.at[b]),
                (new_m_ref.at[b], new_m_out.at[b]),
                (new_v_ref.at[b], new_v_out.at[b]),
                (new_carry_ref.at[b], new_carry_out.at[b]),
            ],
            sems.at[b],
        )
    for copy in copies:
        copy.wait()


def flatten_rows(given_ref, rows_ref):
    steps, width = given_ref.shape[1:]
    strip = 512
    for c in range(0, width, strip):
        rows_ref[:, c : c + strip] = given_ref[:, :, c : c + strip].reshape(-1, strip)


def add_delta_product(groups, rows, blocks_ref, base_ref, out_ref):
    tile = blocks_ref.shape[-1]
    across = base_ref.shape[1] // tile
    deep = rows.shape[1] // tile // groups
    width = deep * tile
    total = jnp.zeros(base_ref.shape, jnp.float32)
    for k in range(groups):
        weights = jnp.concatenate(
            [
                jnp.concatenate([blocks_ref[r * across + c] for c in range(across)], axis=1)
                for r in range(k * deep, (k + 1) * deep)
            ],
            axis=0,
        )
        total += jnp.dot(
            rows[:, k * width : (k + 1) * width], weights, preferred_element_type=jnp.float32
        )
    total = base_ref[...] + total * (1.0 / wire_scale)
    out_ref[...] = total.astype(out_ref.dtype).reshape(out_ref.shape)


def in_hbm(x):
    return pltpu.with_memory_space_constraint(x, pltpu.HBM)


def in_vmem(x):
    return pltpu.with_memory_space_constraint(x, pltpu.VMEM)


def grant(mib):
    return pltpu.CompilerParams(vmem_limit_bytes=mib * 1024 * 1024)


def on_device(
    grad_parts,
    master,
    m_state,
    v_state,
    residual_carry,
    sel_counts,
    sel_order,
    rollout_weight,
    decode_in,
):
    tile_size = grad_parts.shape[-1]
    size = grad_parts.shape[1]
    parts = in_hbm(grad_parts.reshape(size, -1, tile_size, tile_size))
    owned = parts.shape[1:]
    sums = jax.ShapeDtypeStruct(owned, parts.dtype)
    pairs = jax.ShapeDtypeStruct((2,) + owned, parts.dtype)
    here = lax.axis_index("dp").reshape(1)

    far, up, down = pl.pallas_call(
        pack_first_round,
        out_shape=(sums, pairs, pairs),
        in_specs=[SMEM, ANY],
        out_specs=(VMEM, VMEM, VMEM),
        scratch_shapes=[pltpu.SemaphoreType.DMA((5,))],
        compiler_params=grant(4),
        name="pack_first_round",
    )(here, parts)
    opposite = [(i, (i + 2) % size if i % 2 == 0 else (i - 2) % size) for i in range(size)]
    far = lax.ppermute(far, "dp", opposite)
    up = lax.ppermute(up, "dp", shifted(size, 1))
    down = lax.ppermute(down, "dp", shifted(size, -1))
    up_two, down_two = pl.pallas_call(
        pack_second_round,
        out_shape=(sums, sums),
        in_specs=[SMEM, ANY, ANY, ANY, ANY],
        out_specs=(VMEM, VMEM),
        scratch_shapes=[
            pltpu.VMEM((5,) + owned, parts.dtype),
            pltpu.SemaphoreType.DMA((5,)),
        ],
        compiler_params=grant(4),
        name="pack_second_round",
    )(here, parts, up, down, far)
    up_two = lax.ppermute(up_two, "dp", shifted(size, 2))
    down_two = lax.ppermute(down_two, "dp", shifted(size, -2))

    near = pl.pallas_call(
        sum_near,
        out_shape=jax.ShapeDtypeStruct(owned, jnp.float32),
        in_specs=[SMEM, ANY, ANY, ANY],
        out_specs=VMEM,
        scratch_shapes=[
            pltpu.VMEM((3,) + owned, parts.dtype),
            pltpu.SemaphoreType.DMA((3,)),
        ],
        compiler_params=grant(4),
        name="sum_near",
    )(here, parts, up, down)
    states = [(owned, x.dtype) for x in (master, m_state, v_state, residual_carry)]
    new_master, new_m, new_v, new_carry, sent = pl.pallas_call(
        adam_and_select,
        out_shape=[jax.ShapeDtypeStruct(*x) for x in states]
        + [jax.ShapeDtypeStruct(owned, jnp.bfloat16)],
        in_specs=[SMEM, SMEM] + [VMEM] * 7,
        out_specs=[ANY] * 4 + [VMEM],
        scratch_shapes=[pltpu.VMEM(*x) for x in states]
        + [pltpu.SemaphoreType.DMA((owned[0], 4))],
        compiler_params=grant(8),
        name="adam_and_select",
    )(
        sel_counts.reshape(-1),
        sel_order.reshape(-1),
        near,
        up_two,
        down_two,
        master.reshape(owned),
        m_state.reshape(owned),
        v_state.reshape(owned),
        residual_carry.reshape(owned),
    )
    sent = (wide(sent) * wire_scale).astype(jnp.float16)
    gathered = lax.all_gather(sent, "fsdp", axis=0, tiled=True)
    gathered = gathered.astype(jnp.bfloat16)

    model_width, group_width = rollout_weight.shape
    given = decode_in.reshape(decode_in.shape[1:])
    rows = pl.pallas_call(
        flatten_rows,
        out_shape=pltpu.VMEM((given.shape[0] * given.shape[1], model_width), given.dtype),
        in_specs=[VMEM],
        out_specs=VMEM,
        compiler_params=grant(24),
        name="flatten_rows",
    )(given)
    base = jnp.dot(rows, rollout_weight, preferred_element_type=jnp.float32)
    groups = 8
    decode_out = pl.pallas_call(
        functools.partial(add_delta_product, groups),
        out_shape=jax.ShapeDtypeStruct(
            (decode_in.shape[1], decode_in.shape[2], group_width), jnp.bfloat16
        ),
        in_specs=[VMEM, VMEM, VMEM],
        out_specs=VMEM,
        compiler_params=grant(12),
        name="add_delta_product",
    )(rows, gathered, base)
    return (
        new_master.reshape(master.shape),
        new_m.reshape(m_state.shape),
        new_v.reshape(v_state.shape),
        new_carry.reshape(residual_carry.shape),
        decode_out.reshape(decode_in.shape[:3] + (group_width,)),
    )


def solution(mesh):
    return jax.shard_map(
        on_device,
        mesh=mesh,
        in_specs=(
            P("dp", None, "tensor", "fsdp", None, None, None),
            P("dp", "tensor", "fsdp", None, None, None),
            P("dp", "tensor", "fsdp", None, None, None),
            P("dp", "tensor", "fsdp", None, None, None),
            P("dp", "tensor", "fsdp", None, None, None),
            P("dp", "tensor", "fsdp"),
            P("dp", "tensor", "fsdp", None),
            P(None, ("dp", "tensor")),
            P("fsdp", None, None, None),
        ),
        out_specs=(
            P("dp", "tensor", "fsdp", None, None, None),
            P("dp", "tensor", "fsdp", None, None, None),
            P("dp", "tensor", "fsdp", None, None, None),
            P("dp", "tensor", "fsdp", None, None, None),
            P("fsdp", None, None, ("dp", "tensor")),
        ),
        check_vma=False,
    )
```

time: 92 us -> 79.5 us (0.86)
  other arithmetic: 10.9 us -> 0.63 us
  local copies, waits for them, and re-layouts: 9.97 us -> 1.96 us
  Pallas kernels: 1.16 us -> 7.65 us
  waiting for transfers between devices: 3.97 us -> 6.38 us
  matrix products: 2.97 us -> 1.01 us
  blocking collectives: 32 us -> 30.8 us
    reshape x2 -> x0, local copies, waits for them, and re-layouts: 6.67 us -> none  [the longest x1 5.96 us: on_device(): flat_rows = decode_in.reshape(-1, model_width)]
    pallas_call x1 -> x6, Pallas kernels: 1.16 us -> 7.65 us  [the longest x1 1.87 us: on_device(): pl.pallas_call(functools.partial(add_delta_product, groups), out_shape=ja...]
    convert_element_type x4 -> x2, other arithmetic: 7.12 us -> 0.63 us  [the longest x1 0.59 us: on_device(): gathered = gathered.astype(jnp.bfloat16)]
    ppermute x5, waiting for transfers between devices: 3.97 us -> 6.38 us  [the longest x1 5.59 us: on_device(): far = lax.ppermute(far, 'dp', opposite)]
    dynamic_slice x1 -> x0, local copies, waits for them, and re-layouts: 2.14 us -> none  [part(): lax.dynamic_index_in_dim(parts, (here + places) % size, 0, keepdims=False)]
    unnamed x1 -> x0, other arithmetic: 2.13 us -> none
    dot_general x1, matrix products: 2.97 us -> 1.01 us  [on_device(): base = jnp.dot(rows, rollout_weight, preferred_element_type=jnp.float32)]
    another operation x2 -> x0, other arithmetic: 1.51 us -> none  [the longest x1 0.76 us: sum_at_owner(): up = lax.ppermute(jnp.stack([part(3), part(1)]), 'dp', shifted(size, 1))]
  transfers between devices with their start and end apart: 5 -> 5, of which waited for: 2 -> 2; matrix products, arithmetic and copies ran while one was open for 11% -> 1% of each run, Pallas kernels for 0% -> 2%
where the time goes in v2:
time: 79.5 us; the launch traced here: 79.2 us
  blocking collectives  30.8 us (39%)
  starting transfers between devices  29.2 us (37%)
  Pallas kernels  7.65 us (10%)
  waiting for transfers between devices  6.38 us (8%)
  local copies, waits for them, and re-layouts  1.96 us (2%)
  between operations  1.47 us (2%)
  matrix products  1.01 us (1%)
    all_gather x1, blocking collectives, on_device(): gathered = lax.all_gather(sent, 'fsdp', axis=0, tiled=True)  30.8 us
    ppermute x1, starting transfers between devices, on_device(): down = lax.ppermute(down, 'dp', shifted(size, -1))  14 us
    ppermute x1, starting transfers between devices, on_device(): up = lax.ppermute(up, 'dp', shifted(size, 1))  5.74 us
    ppermute x1, starting transfers between devices, on_device(): down_two = lax.ppermute(down_two, 'dp', shifted(size, -2))  5.6 us
    ppermute x1, waiting for transfers between devices, on_device(): far = lax.ppermute(far, 'dp', opposite)  5.59 us
    unnamed x14, local copies, waits for them, and re-layouts  1.96 us
    ppermute x1, starting transfers between devices, on_device(): far = lax.ppermute(far, 'dp', opposite)  1.92 us
    ppermute x1, starting transfers between devices, on_device(): up_two = lax.ppermute(up_two, 'dp', shifted(size, 2))  1.92 us
  transfers between devices with their start and end apart: 5, of which 2 were waited for; matrix products, arithmetic and copies ran while one was open for 1% of the time, Pallas kernels for 2%

profile of v2, /device:TPU:1, one launch (start us, length us, event | category | flops | bytes accessed | tf_op | source)
XLA Modules:
  0.0 79.2 jit_solution(17235297333310158499)
XLA Ops:
  0.6 0.0 copy-start
  0.7 1.4 %pack_first_round.1 = (bf16[5,128,128]{2,1,0:T(8,128)(2,1)S(1)}, bf16[2,5,128,128]{3,2,1,0:T(8,128)(2,1)S(1)}, bf16[2,5,128,128]{3,2,1,0:T(8,128)(2,1)S(1)}) custom-call(s32[1]{0:T(128)} %bitcast.2.here_ref, bf16[8,5,128,128]{3,2,1,0:T(8,128)(2,1)} %bitcast.23), custom_call_target="tpu_custom_call" | custom-call | tf_op jit(solution)/shard_map/pack_first_round/pallas_call | solution.py:219
  2.1 5.7 %collective-permute-start = (bf16[2,5,128,128]{3,2,1,0:T(8,128)(2,1)S(1)}, bf16[2,5,128,128]{3,2,1,0:T(8,128)(2,1)S(1)}, u32[]{:S(2)}, u32[]{:S(2)}) collective-permute-start(bf16[2,5,128,128]{3,2,1,0:T(8,128)(2,1)S(1)} %get-tuple-element.15), channel_id=1, source_target_pairs={{0,128},{128,256},{256,384},{384,512},{512,640},{640,768},{768,896... | collective-permute-start | bytes 983048 | tf_op jit(solution)/shard_map/ppermute | solution.py:230
  7.8 14.0 %collective-permute-start.1 = (bf16[2,5,128,128]{3,2,1,0:T(8,128)(2,1)S(1)}, bf16[2,5,128,128]{3,2,1,0:T(8,128)(2,1)S(1)}, u32[]{:S(2)}, u32[]{:S(2)}) collective-permute-start(bf16[2,5,128,128]{3,2,1,0:T(8,128)(2,1)S(1)} %get-tuple-element.16), channel_id=1, source_target_pairs={{0,896},{128,0},{256,128},{384,256},{512,384},{640,512},{768,640},... | collective-permute-start | bytes 983048 | tf_op jit(solution)/shard_map/ppermute | solution.py:231
  21.9 1.9 %collective-permute-start.2 = (bf16[5,128,128]{2,1,0:T(8,128)(2,1)S(1)}, bf16[5,128,128]{2,1,0:T(8,128)(2,1)S(1)}, u32[]{:S(2)}, u32[]{:S(2)}) collective-permute-start(bf16[5,128,128]{2,1,0:T(8,128)(2,1)S(1)} %get-tuple-element.17), channel_id=1, source_target_pairs={{0,256},{128,896},{256,512},{384,128},{512,768},{640,384},{768,0},... | collective-permute-start | bytes 491528 | tf_op jit(solution)/shard_map/ppermute | solution.py:229
  23.8 0.0 copy-start.1
  23.8 1.9 %copy-done.1 = bf16[1,80,4,5120]{3,2,1,0:T(4,128)(2,1)S(1)} copy-done((bf16[1,80,4,5120]{3,2,1,0:T(4,128)(2,1)S(1)}, bf16[1,80,4,5120]{3,2,1,0:T(4,128)(2,1)}, u32[]{:S(2)}) %copy-start.1) | copy-done | bytes 3276824
  25.7 0.4 flatten_rows.1.rows
  26.1 5.6 %collective-permute-done.2.far_ref = bf16[5,128,128]{2,1,0:T(8,128)(2,1)S(1)} collective-permute-done((bf16[5,128,128]{2,1,0:T(8,128)(2,1)S(1)}, bf16[5,128,128]{2,1,0:T(8,128)(2,1)S(1)}, u32[]{:S(2)}, u32[]{:S(2)}) %collective-permute-start.2) | collective-permute-done | bytes 163872 | tf_op jit(solution)/shard_map/ppermute | solution.py:229
  31.7 0.0 collective-permute-done.up_ref
  31.7 0.0 collective-permute-done.1.down_ref
  31.7 1.2 %pack_second_round.1 = (bf16[5,128,128]{2,1,0:T(8,128)(2,1)S(1)}, bf16[5,128,128]{2,1,0:T(8,128)(2,1)S(1)}) custom-call(s32[1]{0:T(128)} %bitcast.2.here_ref, bf16[8,5,128,128]{3,2,1,0:T(8,128)(2,1)} %bitcast.24, bf16[2,5,128,128]{3,2,1,0:T(8,128)(2,1)S(1)} %collective-permute-done.up_ref, bf16[2,5,128,128]{3,2,1,0:T(8,128)(2,1)S(1)} %collective-permute-done.1.down_ref, ...), custom_call_target="tpu_custom_call" | custom-call | tf_op jit(solution)/shard_map/pack_second_round/pallas_call | solution.py:232
  32.9 1.9 %collective-permute-start.3 = (bf16[5,128,128]{2,1,0:T(8,128)(2,1)S(1)}, bf16[5,128,128]{2,1,0:T(8,128)(2,1)S(1)}, u32[]{:S(2)}, u32[]{:S(2)}) collective-permute-start(bf16[5,128,128]{2,1,0:T(8,128)(2,1)S(1)} %get-tuple-element.18), channel_id=1, source_target_pairs={{0,256},{128,384},{256,512},{384,640},{512,768},{640,896},{768,0},... | collective-permute-start | bytes 491528 | tf_op jit(solution)/shard_map/ppermute | solution.py:244
  34.9 0.0 copy-start.2
  34.9 0.0 copy-start.3
  34.9 0.0 copy-start.4
  34.9 0.0 copy-start.5
  34.9 0.0 copy-start.6
  34.9 5.6 %collective-permute-start.4 = (bf16[5,128,128]{2,1,0:T(8,128)(2,1)S(1)}, bf16[5,128,128]{2,1,0:T(8,128)(2,1)S(1)}, u32[]{:S(2)}, u32[]{:S(2)}) collective-permute-start(bf16[5,128,128]{2,1,0:T(8,128)(2,1)S(1)} %get-tuple-element.19), channel_id=1, source_target_pairs={{0,768},{128,896},{256,0},{384,128},{512,256},{640,384},{768,512},... | collective-permute-start | bytes 491528 | tf_op jit(solution)/shard_map/ppermute | solution.py:245
  40.5 0.0 copy-done
  40.5 1.0 %fusion.base_ref = f32[320,256]{1,0:T(8,128)S(1)} fusion(bf16[320,5120]{1,0:T(8,128)(2,1)S(1)} %flatten_rows.1.rows, bf16[5120,256]{1,0:T(8,128)(2,1)S(1)} %copy-done), kind=kOutput, calls=%fused_computation.1 | convolution fusion | flops 838860800 | bytes 6225920 | tf_op jit(solution)/shard_map/dot_general | solution.py:295
  42.2 1.0 %sum_near.1.near_ref = f32[5,128,128]{2,1,0:T(8,128)S(1)} custom-call(s32[1]{0:T(128)} %bitcast.2.here_ref, bf16[8,5,128,128]{3,2,1,0:T(8,128)(2,1)} %bitcast.25, bf16[2,5,128,128]{3,2,1,0:T(8,128)(2,1)S(1)} %collective-permute-done.up_ref, bf16[2,5,128,128]{3,2,1,0:T(8,128)(2,1)S(1)} %collective-permute-done.1.down_ref), custom_call_target="tpu_custom_call" | custom-call | tf_op jit(solution)/shard_map/sum_near/pallas_call | solution.py:247
  43.2 0.0 collective-permute-done.3.up_two_ref
  43.2 0.8 collective-permute-done.4.down_two_ref
  44.0 0.0 copy-done.2
  44.0 0.0 copy-done.3
  44.0 0.0 copy-done.4
  44.0 0.0 copy-done.5
  44.0 0.0 copy-done.6
  44.0 1.8 %adam_and_select.1 = (f32[5,128,128]{2,1,0:T(8,128)}, bf16[5,128,128]{2,1,0:T(8,128)(2,1)}, bf16[5,128,128]{2,1,0:T(8,128)(2,1)}, f32[5,128,128]{2,1,0:T(8,128)}, bf16[5,128,128]{2,1,0:T(8,128)(2,1)S(1)}) custom-call(s32[1]{0:T(128)} %bitcast.16.counts_ref, s32[5]{0:T(128)S(1)} %bitcast.22, f32[5,128,128]{2,1,0:T(8,128)S(1)} %sum_near.1.near_ref, ...), custom_call_target="tpu_custom_call" | custom-call | tf_op jit(solution)/shard_map/adam_and_select/pallas_call | solution.py:260
  45.9 30.8 %all-gather.1 = f16[80,128,128]{2,1,0:T(8,128)(2,1)S(1)} all-gather(f16[5,128,128]{2,1,0:T(8,128)(2,1)S(1)} %multiply_convert_fusion), channel_id=1, replica_groups=mesh['dp'=8,'fsdp'=16,'tensor'=8] {'fsdp'}, dimensions={0}, use_global_device_ids=true | all-gather | bytes 2785280 | tf_op jit(solution)/shard_map/all_gather | solution.py:282
  76.7 0.6 convert_element_type.11.blocks_ref
  77.3 1.9 %add_delta_product.1 = bf16[80,4,256]{2,1,0:T(4,128)(2,1)} custom-call(bf16[320,5120]{1,0:T(8,128)(2,1)S(1)} %flatten_rows.1.rows, bf16[80,128,128]{2,1,0:T(8,128)(2,1)S(1)} %convert_element_type.11.blocks_ref, f32[320,256]{1,0:T(8,128)S(1)} %fusion.base_ref), custom_call_target="tpu_custom_call" | custom-call | tf_op jit(solution)/shard_map/add_delta_product/pallas_call | solution.py:297
  (1 shorter events, 0.0 us)
Async XLA Ops:
  0.6 39.9 %copy-start = (bf16[5120,256]{1,0:T(8,128)(2,1)S(1)}, bf16[5120,256]{1,0:T(8,128)(2,1)}, u32[]{:S(2)}) copy-start(bf16[5120,256]{1,0:T(8,128)(2,1)} %param.16) | copy-start | bytes 7864324
  2.1 29.6 %collective-permute-start = (bf16[2,5,128,128]{3,2,1,0:T(8,128)(2,1)S(1)}, bf16[2,5,128,128]{3,2,1,0:T(8,128)(2,1)S(1)}, u32[]{:S(2)}, u32[]{:S(2)}) collective-permute-start(bf16[2,5,128,128]{3,2,1,0:T(8,128)(2,1)S(1)} %get-tuple-element.15), channel_id=1, source_target_pairs={{0,128},{128,256},{256,384},{384,512},{512,640},{640,768},{768,896... | collective-permute-start | bytes 983048 | tf_op jit(solution)/shard_map/ppermute | solution.py:230
  7.8 23.9 %collective-permute-start.1 = (bf16[2,5,128,128]{3,2,1,0:T(8,128)(2,1)S(1)}, bf16[2,5,128,128]{3,2,1,0:T(8,128)(2,1)S(1)}, u32[]{:S(2)}, u32[]{:S(2)}) collective-permute-start(bf16[2,5,128,128]{3,2,1,0:T(8,128)(2,1)S(1)} %get-tuple-element.16), channel_id=1, source_target_pairs={{0,896},{128,0},{256,128},{384,256},{512,384},{640,512},{768,640},... | collective-permute-start | bytes 983048 | tf_op jit(solution)/shard_map/ppermute | solution.py:231
  21.9 9.8 %collective-permute-start.2 = (bf16[5,128,128]{2,1,0:T(8,128)(2,1)S(1)}, bf16[5,128,128]{2,1,0:T(8,128)(2,1)S(1)}, u32[]{:S(2)}, u32[]{:S(2)}) collective-permute-start(bf16[5,128,128]{2,1,0:T(8,128)(2,1)S(1)} %get-tuple-element.17), channel_id=1, source_target_pairs={{0,256},{128,896},{256,512},{384,128},{512,768},{640,384},{768,0},... | collective-permute-start | bytes 491528 | tf_op jit(solution)/shard_map/ppermute | solution.py:229
  23.8 1.9 %copy-start.1 = (bf16[1,80,4,5120]{3,2,1,0:T(4,128)(2,1)S(1)}, bf16[1,80,4,5120]{3,2,1,0:T(4,128)(2,1)}, u32[]{:S(2)}) copy-start(bf16[1,80,4,5120]{3,2,1,0:T(4,128)(2,1)} %param.17) | copy-start | bytes 9830404
  32.9 10.3 %collective-permute-start.3 = (bf16[5,128,128]{2,1,0:T(8,128)(2,1)S(1)}, bf16[5,128,128]{2,1,0:T(8,128)(2,1)S(1)}, u32[]{:S(2)}, u32[]{:S(2)}) collective-permute-start(bf16[5,128,128]{2,1,0:T(8,128)(2,1)S(1)} %get-tuple-element.18), channel_id=1, source_target_pairs={{0,256},{128,384},{256,512},{384,640},{512,768},{640,896},{768,0},... | collective-permute-start | bytes 491528 | tf_op jit(solution)/shard_map/ppermute | solution.py:244
  34.9 9.2 %copy-start.2 = (f32[1,1,1,5,128,128]{5,4,3,2,1,0:T(8,128)S(1)}, f32[1,1,1,5,128,128]{5,4,3,2,1,0:T(8,128)}, u32[]{:S(2)}) copy-start(f32[1,1,1,5,128,128]{5,4,3,2,1,0:T(8,128)} %param.10) | copy-start | bytes 983044
  34.9 9.1 %copy-start.3 = (f32[1,1,1,5,128,128]{5,4,3,2,1,0:T(8,128)S(1)}, f32[1,1,1,5,128,128]{5,4,3,2,1,0:T(8,128)}, u32[]{:S(2)}) copy-start(f32[1,1,1,5,128,128]{5,4,3,2,1,0:T(8,128)} %param.13) | copy-start | bytes 983044
  34.9 9.1 %copy-start.4 = (bf16[1,1,1,5,128,128]{5,4,3,2,1,0:T(8,128)(2,1)S(1)}, bf16[1,1,1,5,128,128]{5,4,3,2,1,0:T(8,128)(2,1)}, u32[]{:S(2)}) copy-start(bf16[1,1,1,5,128,128]{5,4,3,2,1,0:T(8,128)(2,1)} %param.11) | copy-start | bytes 491524
  34.9 9.1 %copy-start.5 = (bf16[1,1,1,5,128,128]{5,4,3,2,1,0:T(8,128)(2,1)S(1)}, bf16[1,1,1,5,128,128]{5,4,3,2,1,0:T(8,128)(2,1)}, u32[]{:S(2)}) copy-start(bf16[1,1,1,5,128,128]{5,4,3,2,1,0:T(8,128)(2,1)} %param.12) | copy-start | bytes 491524
  34.9 9.1 %copy-start.6 = (s32[1,1,1,5]{3,2,1,0:T(1,128)S(1)}, s32[1,1,1,5]{3,2,1,0:T(1,128)}, u32[]{:S(2)}) copy-start(s32[1,1,1,5]{3,2,1,0:T(1,128)} %param.15) | copy-start | bytes 64
  34.9 9.1 %collective-permute-start.4 = (bf16[5,128,128]{2,1,0:T(8,128)(2,1)S(1)}, bf16[5,128,128]{2,1,0:T(8,128)(2,1)S(1)}, u32[]{:S(2)}, u32[]{:S(2)}) collective-permute-start(bf16[5,128,128]{2,1,0:T(8,128)(2,1)S(1)} %get-tuple-element.19), channel_id=1, source_target_pairs={{0,768},{128,896},{256,0},{384,128},{512,256},{640,384},{768,512},... | collective-permute-start | bytes 491528 | tf_op jit(solution)/shard_map/ppermute | solution.py:245

commit v3 on v2

--- a/solution.py
+++ b/solution.py
@@ -56,45 +56,36 @@
         copy.wait()
 
 
-def pack_second_round(
-    here_ref, parts_ref, up_ref, down_ref, far_ref, up_two_ref, down_two_ref, got, sems
-):
+def stage_own(here_ref, parts_ref, ahead_ref, behind_ref, own_ref, sems):
     size = parts_ref.shape[0]
     here = here_ref[0]
     copies = fetch(
         [
-            (parts_ref.at[lax.rem(here + 2, size)], got.at[0]),
-            (parts_ref.at[lax.rem(here + size - 2, size)], got.at[1]),
-            (up_ref.at[0], got.at[2]),
-            (down_ref.at[0], got.at[3]),
-            (far_ref, got.at[4]),
+            (parts_ref.at[lax.rem(here + 2, size)], ahead_ref),
+            (parts_ref.at[lax.rem(here + size - 2, size)], behind_ref),
+            (parts_ref.at[here], own_ref),
         ],
         sems,
     )
     for copy in copies:
         copy.wait()
-    far = wide(got[4])
-    upward = lax.rem(here, 2) == 0
-    up_two_ref[...] = (
-        wide(got[0]) + wide(got[2]) + jnp.where(upward, far, jnp.zeros_like(far))
-    ).astype(up_two_ref.dtype)
-    down_two_ref[...] = (
-        wide(got[1]) + wide(got[3]) + jnp.where(upward, jnp.zeros_like(far), far)
-    ).astype(down_two_ref.dtype)
-
-
-def sum_near(here_ref, parts_ref, up_ref, down_ref, near_ref, got, sems):
-    copies = fetch(
-        [
-            (parts_ref.at[here_ref[0]], got.at[0]),
-            (up_ref.at[1], got.at[1]),
-            (down_ref.at[1], got.at[2]),
-        ],
-        sems,
-    )
-    for copy in copies:
-        copy.wait()
-    near_ref[...] = wide(got[0]) + wide(got[1]) + wide(got[2])
+
+
+def pack_second_round(
+    here_ref, ahead_ref, behind_ref, up_ref, down_ref, far_ref, up_two_ref, down_two_ref
+):
+    upward = lax.rem(here_ref[0], 2) == 1
+    for b in range(far_ref.shape[0]):
+        far = wide(far_ref[b])
+        none = jnp.zeros_like(far)
+        up_two = wide(ahead_ref[b]) + wide(up_ref[0, b]) + jnp.where(upward, far, none)
+        down_two = wide(behind_ref[b]) + wide(down_ref[0, b]) + jnp.where(upward, none, far)
+        up_two_ref[b] = up_two.astype(up_two_ref.dtype)
+        down_two_ref[b] = down_two.astype(down_two_ref.dtype)
+
+
+def sum_near(own_ref, up_ref, down_ref, near_ref):
+    near_ref[...] = wide(own_ref[...]) + wide(up_ref[1]) + wide(down_ref[1])
 
 
 def adam_and_select(
@@ -107,20 +98,14 @@
     m_ref,
     v_ref,
     residual_ref,
-    new_master_out,
-    new_m_out,
-    new_v_out,
-    new_carry_out,
-    sent_ref,
     new_master_ref,
     new_m_ref,
     new_v_ref,
     new_carry_ref,
-    sems,
+    sent_ref,
 ):
     first_scale = adam_rate / (1.0 - decay_first**adam_count)
     second_scale = 1.0 / (1.0 - decay_second**adam_count)
-    copies = []
     for b in range(near_ref.shape[0]):
         grad_sum = near_ref[b] + wide(up_two_ref[b]) + wide(down_two_ref[b])
         master = master_ref[b]
@@ -144,17 +129,6 @@
         new_master_ref[b] = master - update
         new_m_ref[b] = first.astype(new_m_ref.dtype)
         new_v_ref[b] = second.astype(new_v_ref.dtype)
-        copies += fetch(
-            [
-                (new_master_ref.at[b], new_master_out.at[b]),
-                (new_m_ref.at[b], new_m_out.at[b]),
-                (new_v_ref.at[b], new_v_out.at[b]),
-                (new_carry_ref.at[b], new_carry_out.at[b]),
-            ],
-            sems.at[b],
-        )
-    for copy in copies:
-        copy.wait()
 
 
 def flatten_rows(given_ref, rows_ref):
@@ -164,7 +138,9 @@
         rows_ref[:, c : c + strip] = given_ref[:, :, c : c + strip].reshape(-1, strip)
 
 
-def add_delta_product(groups, rows, blocks_ref, base_ref, out_ref):
+def add_delta_product(groups, rows, blocks_ref, base_ref, *refs):
+    states, out_ref, outs, sems = refs[:4], refs[4], refs[5:9], refs[9]
+    copies = fetch(list(zip(states, outs)), sems)
     tile = blocks_ref.shape[-1]
     across = base_ref.shape[1] // tile
     deep = rows.shape[1] // tile // groups
@@ -183,6 +159,8 @@
         )
     total = base_ref[...] + total * (1.0 / wire_scale)
     out_ref[...] = total.astype(out_ref.dtype).reshape(out_ref.shape)
+    for copy in copies:
+        copy.wait()
 
 
 def in_hbm(x):
@@ -225,46 +203,44 @@
         compiler_params=grant(4),
         name="pack_first_round",
     )(here, parts)
-    opposite = [(i, (i + 2) % size if i % 2 == 0 else (i - 2) % size) for i in range(size)]
+    ahead, behind, own = pl.pallas_call(
+        stage_own,
+        out_shape=[pltpu.VMEM(owned, parts.dtype)] * 3,
+        in_specs=[SMEM, ANY],
+        out_specs=[VMEM] * 3,
+        scratch_shapes=[pltpu.SemaphoreType.DMA((3,))],
+        compiler_params=grant(4),
+        name="stage_own",
+    )(here, parts)
+    opposite = [(i, (i - 2) % size if i % 2 == 0 else (i + 2) % size) for i in range(size)]
     far = lax.ppermute(far, "dp", opposite)
     up = lax.ppermute(up, "dp", shifted(size, 1))
     down = lax.ppermute(down, "dp", shifted(size, -1))
     up_two, down_two = pl.pallas_call(
         pack_second_round,
         out_shape=(sums, sums),
-        in_specs=[SMEM, ANY, ANY, ANY, ANY],
+        in_specs=[SMEM] + [VMEM] * 5,
         out_specs=(VMEM, VMEM),
-        scratch_shapes=[
-            pltpu.VMEM((5,) + owned, parts.dtype),
-            pltpu.SemaphoreType.DMA((5,)),
-        ],
         compiler_params=grant(4),
         name="pack_second_round",
-    )(here, parts, up, down, far)
+    )(here, in_vmem(ahead), in_vmem(behind), up, down, far)
     up_two = lax.ppermute(up_two, "dp", shifted(size, 2))
     down_two = lax.ppermute(down_two, "dp", shifted(size, -2))
 
     near = pl.pallas_call(
         sum_near,
         out_shape=jax.ShapeDtypeStruct(owned, jnp.float32),
-        in_specs=[SMEM, ANY, ANY, ANY],
+        in_specs=[VMEM] * 3,
         out_specs=VMEM,
-        scratch_shapes=[
-            pltpu.VMEM((3,) + owned, parts.dtype),
-            pltpu.SemaphoreType.DMA((3,)),
-        ],
         compiler_params=grant(4),
         name="sum_near",
-    )(here, parts, up, down)
-    states = [(owned, x.dtype) for x in (master, m_state, v_state, residual_carry)]
-    new_master, new_m, new_v, new_carry, sent = pl.pallas_call(
+    )(in_vmem(own), up, down)
+    kinds = [(owned, x.dtype) for x in (master, m_state, v_state, residual_carry)]
+    *states, sent = pl.pallas_call(
         adam_and_select,
-        out_shape=[jax.ShapeDtypeStruct(*x) for x in states]
-        + [jax.ShapeDtypeStruct(owned, jnp.bfloat16)],
+        out_shape=[pltpu.VMEM(*x) for x in kinds] + [jax.ShapeDtypeStruct(owned, jnp.bfloat16)],
         in_specs=[SMEM, SMEM] + [VMEM] * 7,
-        out_specs=[ANY] * 4 + [VMEM],
-        scratch_shapes=[pltpu.VMEM(*x) for x in states]
-        + [pltpu.SemaphoreType.DMA((owned[0], 4))],
+        out_specs=[VMEM] * 5,
         compiler_params=grant(8),
         name="adam_and_select",
     )(
@@ -294,16 +270,20 @@
     )(given)
     base = jnp.dot(rows, rollout_weight, preferred_element_type=jnp.float32)
     groups = 8
-    decode_out = pl.pallas_call(
+    decode_out, new_master, new_m, new_v, new_carry = pl.pallas_call(
         functools.partial(add_delta_product, groups),
-        out_shape=jax.ShapeDtypeStruct(
-            (decode_in.shape[1], decode_in.shape[2], group_width), jnp.bfloat16
-        ),
-        in_specs=[VMEM, VMEM, VMEM],
-        out_specs=VMEM,
+        out_shape=[
+            jax.ShapeDtypeStruct(
+                (decode_in.shape[1], decode_in.shape[2], group_width), jnp.bfloat16
+            )
+        ]
+        + [jax.ShapeDtypeStruct(*x) for x in kinds],
+        in_specs=[VMEM] * 7,
+        out_specs=[VMEM] + [ANY] * 4,
+        scratch_shapes=[pltpu.SemaphoreType.DMA((4,))],
         compiler_params=grant(12),
         name="add_delta_product",
-    )(rows, gathered, base)
+    )(rows, gathered, base, *[in_vmem(x) for x in states])
     return (
         new_master.reshape(master.shape),
         new_m.reshape(m_state.shape),

time: 79.5 us -> 75.5 us (0.950)
  blocking collectives: 30.8 us -> 25.5 us
  starting transfers between devices: 29.2 us -> 31.1 us
  Pallas kernels: 7.65 us -> 6.06 us
  waiting for transfers between devices: 6.38 us -> 7.39 us
    all_gather x1, blocking collectives: 30.8 us -> 25.5 us  [on_device(): gathered = lax.all_gather(sent, 'fsdp', axis=0, tiled=True)]
    ppermute x1, waiting for transfers between devices: 0.78 us -> 4.57 us  [on_device(): down_two = lax.ppermute(down_two, 'dp', shifted(size, -2))]
    ppermute x1, waiting for transfers between devices: 5.59 us -> 2.81 us  [on_device(): far = lax.ppermute(far, 'dp', opposite)]
    ppermute x1, starting transfers between devices: 1.92 us -> 3.09 us  [on_device(): far = lax.ppermute(far, 'dp', opposite)]
    ppermute x1, starting transfers between devices: 1.92 us -> 3.03 us  [on_device(): up_two = lax.ppermute(up_two, 'dp', shifted(size, 2))]
    pallas_call x1, Pallas kernels: 1.01 us -> 0.06 us  [on_device(): pl.pallas_call(sum_near, out_shape=jax.ShapeDtypeStruct(owned, jnp.float3...]
    pallas_call x3 -> x4, Pallas kernels: 4.83 us -> 4.18 us  [the longest x1 2 us: on_device(): pl.pallas_call(functools.partial(add_delta_product, groups), out_shape=[j...]
where the time goes in v3:
time: 75.5 us; the launch traced here: 75.2 us
  starting transfers between devices  31.1 us (41%)
  blocking collectives  25.5 us (34%)
  waiting for transfers between devices  7.39 us (10%)
  Pallas kernels  6.06 us (8%)
  local copies, waits for them, and re-layouts  1.96 us (3%)
  between operations  1.47 us (2%)
  matrix products  1.01 us (1%)
    all_gather x1, blocking collectives, on_device(): gathered = lax.all_gather(sent, 'fsdp', axis=0, tiled=True)  25.5 us
    ppermute x1, starting transfers between devices, on_device(): down = lax.ppermute(down, 'dp', shifted(size, -1))  14 us
    ppermute x1, starting transfers between devices, on_device(): up = lax.ppermute(up, 'dp', shifted(size, 1))  5.74 us
    ppermute x1, starting transfers between devices, on_device(): down_two = lax.ppermute(down_two, 'dp', shifted(size, -2))  5.24 us
    ppermute x1, waiting for transfers between devices, on_device(): down_two = lax.ppermute(down_two, 'dp', shifted(size, -2))  4.57 us
    ppermute x1, starting transfers between devices, on_device(): far = lax.ppermute(far, 'dp', opposite)  3.09 us
    ppermute x1, starting transfers between devices, on_device(): up_two = lax.ppermute(up_two, 'dp', shifted(size, 2))  3.03 us
    ppermute x1, waiting for transfers between devices, on_device(): far = lax.ppermute(far, 'dp', opposite)  2.81 us
  transfers between devices with their start and end apart: 5, of which 2 were waited for; matrix products, arithmetic and copies ran while one was open for 1% of the time, Pallas kernels for 2%

profile of v3, /device:TPU:1, one launch (start us, length us, event | category | flops | bytes accessed | tf_op | source)
XLA Modules:
  0.0 75.2 jit_solution(18059833198928888748)
XLA Ops:
  0.6 0.0 copy-start
  0.7 1.4 %pack_first_round.1 = (bf16[5,128,128]{2,1,0:T(8,128)(2,1)S(1)}, bf16[2,5,128,128]{3,2,1,0:T(8,128)(2,1)S(1)}, bf16[2,5,128,128]{3,2,1,0:T(8,128)(2,1)S(1)}) custom-call(s32[1]{0:T(128)} %bitcast.3.here_ref, bf16[8,5,128,128]{3,2,1,0:T(8,128)(2,1)} %bitcast.23), custom_call_target="tpu_custom_call" | custom-call | tf_op jit(solution)/shard_map/pack_first_round/pallas_call | solution.py:197
  2.1 5.7 %collective-permute-start = (bf16[2,5,128,128]{3,2,1,0:T(8,128)(2,1)S(1)}, bf16[2,5,128,128]{3,2,1,0:T(8,128)(2,1)S(1)}, u32[]{:S(2)}, u32[]{:S(2)}) collective-permute-start(bf16[2,5,128,128]{3,2,1,0:T(8,128)(2,1)S(1)} %get-tuple-element.24), channel_id=1, source_target_pairs={{0,128},{128,256},{256,384},{384,512},{512,640},{640,768},{768,896... | collective-permute-start | bytes 983048 | tf_op jit(solution)/shard_map/ppermute | solution.py:217
  7.8 14.0 %collective-permute-start.1 = (bf16[2,5,128,128]{3,2,1,0:T(8,128)(2,1)S(1)}, bf16[2,5,128,128]{3,2,1,0:T(8,128)(2,1)S(1)}, u32[]{:S(2)}, u32[]{:S(2)}) collective-permute-start(bf16[2,5,128,128]{3,2,1,0:T(8,128)(2,1)S(1)} %get-tuple-element.25), channel_id=1, source_target_pairs={{0,896},{128,0},{256,128},{384,256},{512,384},{640,512},{768,640},... | collective-permute-start | bytes 983048 | tf_op jit(solution)/shard_map/ppermute | solution.py:218
  21.9 3.1 %collective-permute-start.2 = (bf16[5,128,128]{2,1,0:T(8,128)(2,1)S(1)}, bf16[5,128,128]{2,1,0:T(8,128)(2,1)S(1)}, u32[]{:S(2)}, u32[]{:S(2)}) collective-permute-start(bf16[5,128,128]{2,1,0:T(8,128)(2,1)S(1)} %get-tuple-element.28), channel_id=1, source_target_pairs={{0,768},{128,384},{256,0},{384,640},{512,256},{640,896},{768,512},... | collective-permute-start | bytes 491528 | tf_op jit(solution)/shard_map/ppermute | solution.py:216
  25.0 1.1 %stage_own.1 = (bf16[5,128,128]{2,1,0:T(8,128)(2,1)S(1)}, bf16[5,128,128]{2,1,0:T(8,128)(2,1)S(1)}, bf16[5,128,128]{2,1,0:T(8,128)(2,1)S(1)}) custom-call(s32[1]{0:T(128)} %bitcast.3.here_ref, bf16[8,5,128,128]{3,2,1,0:T(8,128)(2,1)} %bitcast.24), custom_call_target="tpu_custom_call" | custom-call | tf_op jit(solution)/shard_map/stage_own/pallas_call | solution.py:206
  26.1 0.0 copy-start.1
  26.1 1.9 %copy-done.1 = bf16[1,80,4,5120]{3,2,1,0:T(4,128)(2,1)S(1)} copy-done((bf16[1,80,4,5120]{3,2,1,0:T(4,128)(2,1)S(1)}, bf16[1,80,4,5120]{3,2,1,0:T(4,128)(2,1)}, u32[]{:S(2)}) %copy-start.1) | copy-done | bytes 3276824
  28.0 0.4 flatten_rows.1.rows
  28.4 2.8 %collective-permute-done.2.far_ref = bf16[5,128,128]{2,1,0:T(8,128)(2,1)S(1)} collective-permute-done((bf16[5,128,128]{2,1,0:T(8,128)(2,1)S(1)}, bf16[5,128,128]{2,1,0:T(8,128)(2,1)S(1)}, u32[]{:S(2)}, u32[]{:S(2)}) %collective-permute-start.2) | collective-permute-done | bytes 163872 | tf_op jit(solution)/shard_map/ppermute | solution.py:216
  31.2 0.0 collective-permute-done.up_ref
  31.2 0.0 collective-permute-done.1.down_ref
  31.2 0.1 pack_second_round.1
  31.4 3.0 %collective-permute-start.3 = (bf16[5,128,128]{2,1,0:T(8,128)(2,1)S(1)}, bf16[5,128,128]{2,1,0:T(8,128)(2,1)S(1)}, u32[]{:S(2)}, u32[]{:S(2)}) collective-permute-start(bf16[5,128,128]{2,1,0:T(8,128)(2,1)S(1)} %get-tuple-element.29), channel_id=1, source_target_pairs={{0,256},{128,384},{256,512},{384,640},{512,768},{640,896},{768,0},... | collective-permute-start | bytes 491528 | tf_op jit(solution)/shard_map/ppermute | solution.py:227
  34.4 0.0 copy-start.2
  34.4 0.0 copy-start.3
  34.4 0.0 copy-start.4
  34.5 0.0 copy-start.5
  34.5 0.0 copy-start.6
  34.5 5.2 %collective-permute-start.4 = (bf16[5,128,128]{2,1,0:T(8,128)(2,1)S(1)}, bf16[5,128,128]{2,1,0:T(8,128)(2,1)S(1)}, u32[]{:S(2)}, u32[]{:S(2)}) collective-permute-start(bf16[5,128,128]{2,1,0:T(8,128)(2,1)S(1)} %get-tuple-element.30), channel_id=1, source_target_pairs={{0,768},{128,896},{256,0},{384,128},{512,256},{640,384},{768,512},... | collective-permute-start | bytes 491528 | tf_op jit(solution)/shard_map/ppermute | solution.py:228
  39.7 0.0 copy-done
  39.7 1.0 %fusion.base_ref = f32[320,256]{1,0:T(8,128)S(1)} fusion(bf16[320,5120]{1,0:T(8,128)(2,1)S(1)} %flatten_rows.1.rows, bf16[5120,256]{1,0:T(8,128)(2,1)S(1)} %copy-done), kind=kOutput, calls=%fused_computation.1 | convolution fusion | flops 838860800 | bytes 6225920 | tf_op jit(solution)/shard_map/dot_general | solution.py:271
  41.4 0.1 sum_near.1.near_ref
  41.5 0.0 collective-permute-done.3.up_two_ref
  41.5 4.6 %collective-permute-done.4.down_two_ref = bf16[5,128,128]{2,1,0:T(8,128)(2,1)S(1)} collective-permute-done((bf16[5,128,128]{2,1,0:T(8,128)(2,1)S(1)}, bf16[5,128,128]{2,1,0:T(8,128)(2,1)S(1)}, u32[]{:S(2)}, u32[]{:S(2)}) %collective-permute-start.4) | collective-permute-done | bytes 163872 | tf_op jit(solution)/shard_map/ppermute | solution.py:228
  46.0 0.0 copy-done.2
  46.0 0.0 copy-done.3
  46.0 0.0 copy-done.4
  46.0 0.0 copy-done.5
  46.1 0.0 copy-done.6
  46.1 0.9 %adam_and_select.1 = (f32[5,128,128]{2,1,0:T(8,128)S(1)}, bf16[5,128,128]{2,1,0:T(8,128)(2,1)S(1)}, bf16[5,128,128]{2,1,0:T(8,128)(2,1)S(1)}, f32[5,128,128]{2,1,0:T(8,128)S(1)}, bf16[5,128,128]{2,1,0:T(8,128)(2,1)S(1)}) custom-call(s32[1]{0:T(128)} %bitcast.16.counts_ref, s32[5]{0:T(128)S(1)} %bitcast.22, f32[5,128,128]{2,1,0:T(8,128)S(1)} %sum_near.1.near_ref, ...), custom_call_target="tpu_custom_call" | custom-call | tf_op jit(solution)/shard_map/adam_and_select/pallas_call | solution.py:239
  47.1 25.5 %all-gather.1 = f16[80,128,128]{2,1,0:T(8,128)(2,1)S(1)} all-gather(f16[5,128,128]{2,1,0:T(8,128)(2,1)S(1)} %multiply_convert_fusion), channel_id=1, replica_groups=mesh['dp'=8,'fsdp'=16,'tensor'=8] {'fsdp'}, dimensions={0}, use_global_device_ids=true | all-gather | bytes 2785280 | tf_op jit(solution)/shard_map/all_gather | solution.py:258
  72.6 0.6 convert_element_type.11.blocks_ref
  73.2 2.0 %add_delta_product.1 = (bf16[80,4,256]{2,1,0:T(4,128)(2,1)}, f32[5,128,128]{2,1,0:T(8,128)}, bf16[5,128,128]{2,1,0:T(8,128)(2,1)}, bf16[5,128,128]{2,1,0:T(8,128)(2,1)}, f32[5,128,128]{2,1,0:T(8,128)}) custom-call(bf16[320,5120]{1,0:T(8,128)(2,1)S(1)} %flatten_rows.1.rows, bf16[80,128,128]{2,1,0:T(8,128)(2,1)S(1)} %convert_element_type.11.blocks_ref, ...), custom_call_target="tpu_custom_call" | custom-call | tf_op jit(solution)/shard_map/add_delta_product/pallas_call | solution.py:273
  (1 shorter events, 0.0 us)
Async XLA Ops:
  0.6 39.1 %copy-start = (bf16[5120,256]{1,0:T(8,128)(2,1)S(1)}, bf16[5120,256]{1,0:T(8,128)(2,1)}, u32[]{:S(2)}) copy-start(bf16[5120,256]{1,0:T(8,128)(2,1)} %param.16) | copy-start | bytes 7864324
  2.1 29.1 %collective-permute-start = (bf16[2,5,128,128]{3,2,1,0:T(8,128)(2,1)S(1)}, bf16[2,5,128,128]{3,2,1,0:T(8,128)(2,1)S(1)}, u32[]{:S(2)}, u32[]{:S(2)}) collective-permute-start(bf16[2,5,128,128]{3,2,1,0:T(8,128)(2,1)S(1)} %get-tuple-element.24), channel_id=1, source_target_pairs={{0,128},{128,256},{256,384},{384,512},{512,640},{640,768},{768,896... | collective-permute-start | bytes 983048 | tf_op jit(solution)/shard_map/ppermute | solution.py:217
  7.8 23.4 %collective-permute-start.1 = (bf16[2,5,128,128]{3,2,1,0:T(8,128)(2,1)S(1)}, bf16[2,5,128,128]{3,2,1,0:T(8,128)(2,1)S(1)}, u32[]{:S(2)}, u32[]{:S(2)}) collective-permute-start(bf16[2,5,128,128]{3,2,1,0:T(8,128)(2,1)S(1)} %get-tuple-element.25), channel_id=1, source_target_pairs={{0,896},{128,0},{256,128},{384,256},{512,384},{640,512},{768,640},... | collective-permute-start | bytes 983048 | tf_op jit(solution)/shard_map/ppermute | solution.py:218
  21.9 9.3 %collective-permute-start.2 = (bf16[5,128,128]{2,1,0:T(8,128)(2,1)S(1)}, bf16[5,128,128]{2,1,0:T(8,128)(2,1)S(1)}, u32[]{:S(2)}, u32[]{:S(2)}) collective-permute-start(bf16[5,128,128]{2,1,0:T(8,128)(2,1)S(1)} %get-tuple-element.28), channel_id=1, source_target_pairs={{0,768},{128,384},{256,0},{384,640},{512,256},{640,896},{768,512},... | collective-permute-start | bytes 491528 | tf_op jit(solution)/shard_map/ppermute | solution.py:216
  26.1 1.9 %copy-start.1 = (bf16[1,80,4,5120]{3,2,1,0:T(4,128)(2,1)S(1)}, bf16[1,80,4,5120]{3,2,1,0:T(4,128)(2,1)}, u32[]{:S(2)}) copy-start(bf16[1,80,4,5120]{3,2,1,0:T(4,128)(2,1)} %param.17) | copy-start | bytes 9830404
  31.4 10.1 %collective-permute-start.3 = (bf16[5,128,128]{2,1,0:T(8,128)(2,1)S(1)}, bf16[5,128,128]{2,1,0:T(8,128)(2,1)S(1)}, u32[]{:S(2)}, u32[]{:S(2)}) collective-permute-start(bf16[5,128,128]{2,1,0:T(8,128)(2,1)S(1)} %get-tuple-element.29), channel_id=1, source_target_pairs={{0,256},{128,384},{256,512},{384,640},{512,768},{640,896},{768,0},... | collective-permute-start | bytes 491528 | tf_op jit(solution)/shard_map/ppermute | solution.py:227
  34.4 11.6 %copy-start.2 = (f32[1,1,1,5,128,128]{5,4,3,2,1,0:T(8,128)S(1)}, f32[1,1,1,5,128,128]{5,4,3,2,1,0:T(8,128)}, u32[]{:S(2)}) copy-start(f32[1,1,1,5,128,128]{5,4,3,2,1,0:T(8,128)} %param.10) | copy-start | bytes 983044
  34.4 11.6 %copy-start.3 = (f32[1,1,1,5,128,128]{5,4,3,2,1,0:T(8,128)S(1)}, f32[1,1,1,5,128,128]{5,4,3,2,1,0:T(8,128)}, u32[]{:S(2)}) copy-start(f32[1,1,1,5,128,128]{5,4,3,2,1,0:T(8,128)} %param.13) | copy-start | bytes 983044
  34.4 11.6 %copy-start.4 = (bf16[1,1,1,5,128,128]{5,4,3,2,1,0:T(8,128)(2,1)S(1)}, bf16[1,1,1,5,128,128]{5,4,3,2,1,0:T(8,128)(2,1)}, u32[]{:S(2)}) copy-start(bf16[1,1,1,5,128,128]{5,4,3,2,1,0:T(8,128)(2,1)} %param.11) | copy-start | bytes 491524
  34.5 11.6 %copy-start.5 = (bf16[1,1,1,5,128,128]{5,4,3,2,1,0:T(8,128)(2,1)S(1)}, bf16[1,1,1,5,128,128]{5,4,3,2,1,0:T(8,128)(2,1)}, u32[]{:S(2)}) copy-start(bf16[1,1,1,5,128,128]{5,4,3,2,1,0:T(8,128)(2,1)} %param.12) | copy-start | bytes 491524
  34.5 11.6 %copy-start.6 = (s32[1,1,1,5]{3,2,1,0:T(1,128)S(1)}, s32[1,1,1,5]{3,2,1,0:T(1,128)}, u32[]{:S(2)}) copy-start(s32[1,1,1,5]{3,2,1,0:T(1,128)} %param.15) | copy-start | bytes 64
  34.5 11.6 %collective-permute-start.4 = (bf16[5,128,128]{2,1,0:T(8,128)(2,1)S(1)}, bf16[5,128,128]{2,1,0:T(8,128)(2,1)S(1)}, u32[]{:S(2)}, u32[]{:S(2)}) collective-permute-start(bf16[5,128,128]{2,1,0:T(8,128)(2,1)S(1)} %get-tuple-element.30), channel_id=1, source_target_pairs={{0,768},{128,896},{256,0},{384,128},{512,256},{640,384},{768,512},... | collective-permute-start | bytes 491528 | tf_op jit(solution)/shard_map/ppermute | solution.py:228

commit v4 on v3

--- a/solution.py
+++ b/solution.py
@@ -71,29 +71,41 @@
         copy.wait()
 
 
-def pack_second_round(
-    here_ref, ahead_ref, behind_ref, up_ref, down_ref, far_ref, up_two_ref, down_two_ref
-):
-    upward = lax.rem(here_ref[0], 2) == 1
-    for b in range(far_ref.shape[0]):
-        far = wide(far_ref[b])
-        none = jnp.zeros_like(far)
-        up_two = wide(ahead_ref[b]) + wide(up_ref[0, b]) + jnp.where(upward, far, none)
-        down_two = wide(behind_ref[b]) + wide(down_ref[0, b]) + jnp.where(upward, none, far)
-        up_two_ref[b] = up_two.astype(up_two_ref.dtype)
-        down_two_ref[b] = down_two.astype(down_two_ref.dtype)
-
-
-def sum_near(own_ref, up_ref, down_ref, near_ref):
+def pack_plain(here_ref, ahead_ref, behind_ref, up_ref, down_ref, plain_ref):
+    odd = lax.rem(here_ref[0], 2) == 1
+    for b in range(plain_ref.shape[0]):
+        upward = wide(ahead_ref[b]) + wide(up_ref[0, b])
+        downward = wide(behind_ref[b]) + wide(down_ref[0, b])
+        plain_ref[b] = jnp.where(odd, downward, upward).astype(plain_ref.dtype)
+
+
+def pack_joined(here_ref, ahead_ref, behind_ref, up_ref, down_ref, far_ref, joined_ref):
+    odd = lax.rem(here_ref[0], 2) == 1
+    for b in range(joined_ref.shape[0]):
+        upward = wide(ahead_ref[b]) + wide(up_ref[0, b])
+        downward = wide(behind_ref[b]) + wide(down_ref[0, b])
+        joined = jnp.where(odd, upward, downward) + wide(far_ref[b])
+        joined_ref[b] = joined.astype(joined_ref.dtype)
+
+
+def sum_near(counts_ref, order_ref, own_ref, up_ref, down_ref, near_ref, chosen_ref):
     near_ref[...] = wide(own_ref[...]) + wide(up_ref[1]) + wide(down_ref[1])
+    for b in range(near_ref.shape[0]):
+        chosen = functools.reduce(
+            jnp.logical_or,
+            [
+                jnp.logical_and(s < counts_ref[0], order_ref[s] == b)
+                for s in range(order_ref.shape[0])
+            ],
+        )
+        chosen_ref[b] = jnp.full(chosen_ref.shape[1:], chosen.astype(jnp.float32))
 
 
 def adam_and_select(
-    counts_ref,
-    order_ref,
+    chosen_ref,
     near_ref,
-    up_two_ref,
-    down_two_ref,
+    plain_ref,
+    joined_ref,
     master_ref,
     m_ref,
     v_ref,
@@ -107,7 +119,7 @@
     first_scale = adam_rate / (1.0 - decay_first**adam_count)
     second_scale = 1.0 / (1.0 - decay_second**adam_count)
     for b in range(near_ref.shape[0]):
-        grad_sum = near_ref[b] + wide(up_two_ref[b]) + wide(down_two_ref[b])
+        grad_sum = near_ref[b] + wide(plain_ref[b]) + wide(joined_ref[b])
         master = master_ref[b]
         first = decay_first * wide(m_ref[b]) + (1.0 - decay_first) * grad_sum
         second = decay_second * wide(v_ref[b]) + (1.0 - decay_second) * grad_sum * grad_sum
@@ -115,15 +127,8 @@
             jnp.sqrt(second * second_scale) + adam_epsilon
         ) + (adam_rate * weight_decay) * master
         accumulated = residual_ref[b] - update
-        chosen = functools.reduce(
-            jnp.logical_or,
-            [
-                jnp.logical_and(s < counts_ref[0], order_ref[s] == b)
-                for s in range(order_ref.shape[0])
-            ],
-        )
         outbound = accumulated.astype(sent_ref.dtype)
-        outbound = jnp.where(chosen, wide(outbound), jnp.zeros_like(accumulated))
+        outbound = jnp.where(chosen_ref[b] > 0.5, wide(outbound), jnp.zeros_like(accumulated))
         sent_ref[b] = outbound.astype(sent_ref.dtype)
         new_carry_ref[b] = accumulated - outbound
         new_master_ref[b] = master - update
@@ -216,39 +221,48 @@
     far = lax.ppermute(far, "dp", opposite)
     up = lax.ppermute(up, "dp", shifted(size, 1))
     down = lax.ppermute(down, "dp", shifted(size, -1))
-    up_two, down_two = pl.pallas_call(
-        pack_second_round,
-        out_shape=(sums, sums),
+    alike = [(i, (i + 2) % size if i % 2 == 0 else (i - 2) % size) for i in range(size)]
+    ahead, behind = in_vmem(ahead), in_vmem(behind)
+    plain = pl.pallas_call(
+        pack_plain,
+        out_shape=sums,
+        in_specs=[SMEM] + [VMEM] * 4,
+        out_specs=VMEM,
+        compiler_params=grant(4),
+        name="pack_plain",
+    )(here, ahead, behind, up, down)
+    plain = lax.ppermute(plain, "dp", alike)
+    joined = pl.pallas_call(
+        pack_joined,
+        out_shape=sums,
         in_specs=[SMEM] + [VMEM] * 5,
-        out_specs=(VMEM, VMEM),
-        compiler_params=grant(4),
-        name="pack_second_round",
-    )(here, in_vmem(ahead), in_vmem(behind), up, down, far)
-    up_two = lax.ppermute(up_two, "dp", shifted(size, 2))
-    down_two = lax.ppermute(down_two, "dp", shifted(size, -2))
-
-    near = pl.pallas_call(
+        out_specs=VMEM,
+        compiler_params=grant(4),
+        name="pack_joined",
+    )(here, ahead, behind, up, down, far)
+    joined = lax.ppermute(joined, "dp", opposite)
+
+    near, chosen = pl.pallas_call(
         sum_near,
-        out_shape=jax.ShapeDtypeStruct(owned, jnp.float32),
-        in_specs=[VMEM] * 3,
-        out_specs=VMEM,
+        out_shape=[pltpu.VMEM(owned, jnp.float32), pltpu.VMEM((owned[0], 1, tile_size), jnp.float32)],
+        in_specs=[SMEM, SMEM] + [VMEM] * 3,
+        out_specs=[VMEM] * 2,
         compiler_params=grant(4),
         name="sum_near",
-    )(in_vmem(own), up, down)
+    )(sel_counts.reshape(-1), sel_order.reshape(-1), in_vmem(own), up, down)
     kinds = [(owned, x.dtype) for x in (master, m_state, v_state, residual_carry)]
     *states, sent = pl.pallas_call(
         adam_and_select,
         out_shape=[pltpu.VMEM(*x) for x in kinds] + [jax.ShapeDtypeStruct(owned, jnp.bfloat16)],
-        in_specs=[SMEM, SMEM] + [VMEM] * 7,
+        in_specs=[VMEM] * 8,
         out_specs=[VMEM] * 5,
         compiler_params=grant(8),
         name="adam_and_select",
     )(
-        sel_counts.reshape(-1),
-        sel_order.reshape(-1),
-        near,
-        up_two,
-        down_two,
+        in_vmem(chosen),
+        in_vmem(near),
+        plain,
+        joined,
         master.reshape(owned),
         m_state.reshape(owned),
         v_state.reshape(owned),

time: 75.5 us -> 73.8 us (0.977)
  waiting for transfers between devices: 7.39 us -> 0.22 us
  blocking collectives: 25.5 us -> 30.1 us
  starting transfers between devices: 31.1 us -> 31.9 us
    all_gather x1, blocking collectives: 25.5 us -> 30.1 us  [on_device(): gathered = lax.all_gather(sent, 'fsdp', axis=0, tiled=True)]
    ppermute x2, waiting for transfers between devices: 4.57 us -> 0.21 us  [the longest x1 0.21 us: on_device(): joined = lax.ppermute(joined, 'dp', opposite)]
    ppermute x1, waiting for transfers between devices: 2.81 us -> 0.01 us  [on_device(): far = lax.ppermute(far, 'dp', opposite)]
  transfers between devices with their start and end apart: 5 -> 5, of which waited for: 2 -> 1; matrix products, arithmetic and copies ran while one was open for 1% -> 1% of each run, Pallas kernels for 2% -> 3%
where the time goes in v4:
time: 73.8 us; the launch traced here: 73.5 us
  starting transfers between devices  31.9 us (43%)
  blocking collectives  30.1 us (41%)
  Pallas kernels  6.13 us (8%)
  local copies, waits for them, and re-layouts  1.96 us (3%)
  between operations  1.5 us (2%)
  matrix products  1.01 us (1%)
    all_gather x1, blocking collectives, on_device(): gathered = lax.all_gather(sent, 'fsdp', axis=0, tiled=True)  30.1 us
    ppermute x1, starting transfers between devices, on_device(): down = lax.ppermute(down, 'dp', shifted(size, -1))  14 us
    ppermute x1, starting transfers between devices, on_device(): joined = lax.ppermute(joined, 'dp', opposite)  5.93 us
    ppermute x1, starting transfers between devices, on_device(): up = lax.ppermute(up, 'dp', shifted(size, 1))  5.74 us
    ppermute x1, starting transfers between devices, on_device(): far = lax.ppermute(far, 'dp', opposite)  3.09 us
    ppermute x1, starting transfers between devices, on_device(): plain = lax.ppermute(plain, 'dp', alike)  3.09 us
    pallas_call x1, Pallas kernels, on_device(): pl.pallas_call(functools.partial(add_delta_product, groups), out_shape=[j...  2.01 us
    unnamed x14, local copies, waits for them, and re-layouts  1.96 us
  transfers between devices with their start and end apart: 5, of which 1 were waited for; matrix products, arithmetic and copies ran while one was open for 1% of the time, Pallas kernels for 3%

profile of v4, /device:TPU:1, one launch (start us, length us, event | category | flops | bytes accessed | tf_op | source)
XLA Modules:
  0.0 73.5 jit_solution(10982013823397956154)
XLA Ops:
  0.6 0.0 copy-start
  0.7 1.4 %pack_first_round.1 = (bf16[5,128,128]{2,1,0:T(8,128)(2,1)S(1)}, bf16[2,5,128,128]{3,2,1,0:T(8,128)(2,1)S(1)}, bf16[2,5,128,128]{3,2,1,0:T(8,128)(2,1)S(1)}) custom-call(s32[1]{0:T(128)} %bitcast.3.here_ref, bf16[8,5,128,128]{3,2,1,0:T(8,128)(2,1)} %bitcast.23), custom_call_target="tpu_custom_call" | custom-call | tf_op jit(solution)/shard_map/pack_first_round/pallas_call | solution.py:202
  2.1 5.7 %collective-permute-start = (bf16[2,5,128,128]{3,2,1,0:T(8,128)(2,1)S(1)}, bf16[2,5,128,128]{3,2,1,0:T(8,128)(2,1)S(1)}, u32[]{:S(2)}, u32[]{:S(2)}) collective-permute-start(bf16[2,5,128,128]{3,2,1,0:T(8,128)(2,1)S(1)} %get-tuple-element.24), channel_id=1, source_target_pairs={{0,128},{128,256},{256,384},{384,512},{512,640},{640,768},{768,896... | collective-permute-start | bytes 983048 | tf_op jit(solution)/shard_map/ppermute | solution.py:222
  7.8 14.0 %collective-permute-start.1 = (bf16[2,5,128,128]{3,2,1,0:T(8,128)(2,1)S(1)}, bf16[2,5,128,128]{3,2,1,0:T(8,128)(2,1)S(1)}, u32[]{:S(2)}, u32[]{:S(2)}) collective-permute-start(bf16[2,5,128,128]{3,2,1,0:T(8,128)(2,1)S(1)} %get-tuple-element.25), channel_id=1, source_target_pairs={{0,896},{128,0},{256,128},{384,256},{512,384},{640,512},{768,640},... | collective-permute-start | bytes 983048 | tf_op jit(solution)/shard_map/ppermute | solution.py:223
  21.9 3.1 %collective-permute-start.3 = (bf16[5,128,128]{2,1,0:T(8,128)(2,1)S(1)}, bf16[5,128,128]{2,1,0:T(8,128)(2,1)S(1)}, u32[]{:S(2)}, u32[]{:S(2)}) collective-permute-start(bf16[5,128,128]{2,1,0:T(8,128)(2,1)S(1)} %get-tuple-element.30), channel_id=1, source_target_pairs={{0,768},{128,384},{256,0},{384,640},{512,256},{640,896},{768,512},... | collective-permute-start | bytes 491528 | tf_op jit(solution)/shard_map/ppermute | solution.py:221
  25.0 1.1 %stage_own.1 = (bf16[5,128,128]{2,1,0:T(8,128)(2,1)S(1)}, bf16[5,128,128]{2,1,0:T(8,128)(2,1)S(1)}, bf16[5,128,128]{2,1,0:T(8,128)(2,1)S(1)}) custom-call(s32[1]{0:T(128)} %bitcast.3.here_ref, bf16[8,5,128,128]{3,2,1,0:T(8,128)(2,1)} %bitcast.24), custom_call_target="tpu_custom_call" | custom-call | tf_op jit(solution)/shard_map/stage_own/pallas_call | solution.py:211
  26.1 0.0 copy-start.1
  26.1 1.9 %copy-done.1 = bf16[1,80,4,5120]{3,2,1,0:T(4,128)(2,1)S(1)} copy-done((bf16[1,80,4,5120]{3,2,1,0:T(4,128)(2,1)S(1)}, bf16[1,80,4,5120]{3,2,1,0:T(4,128)(2,1)}, u32[]{:S(2)}) %copy-start.1) | copy-done | bytes 3276824
  28.0 0.4 flatten_rows.1.rows
  28.4 0.0 collective-permute-done.up_ref
  28.4 0.0 collective-permute-done.1.down_ref
  28.4 0.1 pack_plain.1
  28.5 3.1 %collective-permute-start.2 = (bf16[5,128,128]{2,1,0:T(8,128)(2,1)S(1)}, bf16[5,128,128]{2,1,0:T(8,128)(2,1)S(1)}, u32[]{:S(2)}, u32[]{:S(2)}) collective-permute-start(bf16[5,128,128]{2,1,0:T(8,128)(2,1)S(1)} %pack_plain.1), channel_id=1, source_target_pairs={{0,256},{128,896},{256,512},{384,128},{512,768},{640,384},{768,0},... | collective-permute-start | bytes 491528 | tf_op jit(solution)/shard_map/ppermute | solution.py:234
  31.6 0.0 collective-permute-done.3.far_ref
  31.6 0.1 pack_joined.1
  31.8 0.0 copy-start.6
  31.8 0.0 copy-start.2
  31.8 0.0 copy-start.3
  31.8 0.0 copy-start.4
  31.8 0.0 copy-start.5
  31.8 5.9 %collective-permute-start.4 = (bf16[5,128,128]{2,1,0:T(8,128)(2,1)S(1)}, bf16[5,128,128]{2,1,0:T(8,128)(2,1)S(1)}, u32[]{:S(2)}, u32[]{:S(2)}) collective-permute-start(bf16[5,128,128]{2,1,0:T(8,128)(2,1)S(1)} %pack_joined.1), channel_id=1, source_target_pairs={{0,768},{128,384},{256,0},{384,640},{512,256},{640,896},{768,512},... | collective-permute-start | bytes 491528 | tf_op jit(solution)/shard_map/ppermute | solution.py:243
  37.8 0.0 copy-done
  37.8 1.0 %fusion.base_ref = f32[320,256]{1,0:T(8,128)S(1)} fusion(bf16[320,5120]{1,0:T(8,128)(2,1)S(1)} %flatten_rows.1.rows, bf16[5120,256]{1,0:T(8,128)(2,1)S(1)} %copy-done), kind=kOutput, calls=%fused_computation.1 | convolution fusion | flops 838860800 | bytes 6225920 | tf_op jit(solution)/shard_map/dot_general | solution.py:285
  39.4 0.0 copy-done.6
  39.4 0.6 sum_near.1
  40.0 0.0 collective-permute-done.2.plain_ref
  40.1 0.2 collective-permute-done.4.joined_ref
  40.3 0.0 copy-done.2
  40.3 0.0 copy-done.3
  40.3 0.0 copy-done.4
  40.3 0.0 copy-done.5
  40.3 0.4 adam_and_select.1
  40.7 30.1 %all-gather.1 = f16[80,128,128]{2,1,0:T(8,128)(2,1)S(1)} all-gather(f16[5,128,128]{2,1,0:T(8,128)(2,1)S(1)} %multiply_convert_fusion), channel_id=1, replica_groups=mesh['dp'=8,'fsdp'=16,'tensor'=8] {'fsdp'}, dimensions={0}, use_global_device_ids=true | all-gather | bytes 2785280 | tf_op jit(solution)/shard_map/all_gather | solution.py:272
  70.9 0.6 convert_element_type.11.blocks_ref
  71.5 2.0 %add_delta_product.1 = (bf16[80,4,256]{2,1,0:T(4,128)(2,1)}, f32[5,128,128]{2,1,0:T(8,128)}, bf16[5,128,128]{2,1,0:T(8,128)(2,1)}, bf16[5,128,128]{2,1,0:T(8,128)(2,1)}, f32[5,128,128]{2,1,0:T(8,128)}) custom-call(bf16[320,5120]{1,0:T(8,128)(2,1)S(1)} %flatten_rows.1.rows, bf16[80,128,128]{2,1,0:T(8,128)(2,1)S(1)} %convert_element_type.11.blocks_ref, ...), custom_call_target="tpu_custom_call" | custom-call | tf_op jit(solution)/shard_map/add_delta_product/pallas_call | solution.py:287
  (1 shorter events, 0.0 us)
Async XLA Ops:
  0.6 37.1 %copy-start = (bf16[5120,256]{1,0:T(8,128)(2,1)S(1)}, bf16[5120,256]{1,0:T(8,128)(2,1)}, u32[]{:S(2)}) copy-start(bf16[5120,256]{1,0:T(8,128)(2,1)} %param.16) | copy-start | bytes 7864324
  2.1 26.3 %collective-permute-start = (bf16[2,5,128,128]{3,2,1,0:T(8,128)(2,1)S(1)}, bf16[2,5,128,128]{3,2,1,0:T(8,128)(2,1)S(1)}, u32[]{:S(2)}, u32[]{:S(2)}) collective-permute-start(bf16[2,5,128,128]{3,2,1,0:T(8,128)(2,1)S(1)} %get-tuple-element.24), channel_id=1, source_target_pairs={{0,128},{128,256},{256,384},{384,512},{512,640},{640,768},{768,896... | collective-permute-start | bytes 983048 | tf_op jit(solution)/shard_map/ppermute | solution.py:222
  7.8 20.6 %collective-permute-start.1 = (bf16[2,5,128,128]{3,2,1,0:T(8,128)(2,1)S(1)}, bf16[2,5,128,128]{3,2,1,0:T(8,128)(2,1)S(1)}, u32[]{:S(2)}, u32[]{:S(2)}) collective-permute-start(bf16[2,5,128,128]{3,2,1,0:T(8,128)(2,1)S(1)} %get-tuple-element.25), channel_id=1, source_target_pairs={{0,896},{128,0},{256,128},{384,256},{512,384},{640,512},{768,640},... | collective-permute-start | bytes 983048 | tf_op jit(solution)/shard_map/ppermute | solution.py:223
  21.9 9.8 %collective-permute-start.3 = (bf16[5,128,128]{2,1,0:T(8,128)(2,1)S(1)}, bf16[5,128,128]{2,1,0:T(8,128)(2,1)S(1)}, u32[]{:S(2)}, u32[]{:S(2)}) collective-permute-start(bf16[5,128,128]{2,1,0:T(8,128)(2,1)S(1)} %get-tuple-element.30), channel_id=1, source_target_pairs={{0,768},{128,384},{256,0},{384,640},{512,256},{640,896},{768,512},... | collective-permute-start | bytes 491528 | tf_op jit(solution)/shard_map/ppermute | solution.py:221
  26.1 1.9 %copy-start.1 = (bf16[1,80,4,5120]{3,2,1,0:T(4,128)(2,1)S(1)}, bf16[1,80,4,5120]{3,2,1,0:T(4,128)(2,1)}, u32[]{:S(2)}) copy-start(bf16[1,80,4,5120]{3,2,1,0:T(4,128)(2,1)} %param.17) | copy-start | bytes 9830404
  28.5 11.5 %collective-permute-start.2 = (bf16[5,128,128]{2,1,0:T(8,128)(2,1)S(1)}, bf16[5,128,128]{2,1,0:T(8,128)(2,1)S(1)}, u32[]{:S(2)}, u32[]{:S(2)}) collective-permute-start(bf16[5,128,128]{2,1,0:T(8,128)(2,1)S(1)} %pack_plain.1), channel_id=1, source_target_pairs={{0,256},{128,896},{256,512},{384,128},{512,768},{640,384},{768,0},... | collective-permute-start | bytes 491528 | tf_op jit(solution)/shard_map/ppermute | solution.py:234
  31.8 7.7 %copy-start.6 = (s32[1,1,1,5]{3,2,1,0:T(1,128)S(1)}, s32[1,1,1,5]{3,2,1,0:T(1,128)}, u32[]{:S(2)}) copy-start(s32[1,1,1,5]{3,2,1,0:T(1,128)} %param.15) | copy-start | bytes 64
  31.8 8.5 %copy-start.2 = (f32[1,1,1,5,128,128]{5,4,3,2,1,0:T(8,128)S(1)}, f32[1,1,1,5,128,128]{5,4,3,2,1,0:T(8,128)}, u32[]{:S(2)}) copy-start(f32[1,1,1,5,128,128]{5,4,3,2,1,0:T(8,128)} %param.10) | copy-start | bytes 983044
  31.8 8.5 %copy-start.3 = (f32[1,1,1,5,128,128]{5,4,3,2,1,0:T(8,128)S(1)}, f32[1,1,1,5,128,128]{5,4,3,2,1,0:T(8,128)}, u32[]{:S(2)}) copy-start(f32[1,1,1,5,128,128]{5,4,3,2,1,0:T(8,128)} %param.13) | copy-start | bytes 983044
  31.8 8.5 %copy-start.4 = (bf16[1,1,1,5,128,128]{5,4,3,2,1,0:T(8,128)(2,1)S(1)}, bf16[1,1,1,5,128,128]{5,4,3,2,1,0:T(8,128)(2,1)}, u32[]{:S(2)}) copy-start(bf16[1,1,1,5,128,128]{5,4,3,2,1,0:T(8,128)(2,1)} %param.11) | copy-start | bytes 491524
  31.8 8.5 %copy-start.5 = (bf16[1,1,1,5,128,128]{5,4,3,2,1,0:T(8,128)(2,1)S(1)}, bf16[1,1,1,5,128,128]{5,4,3,2,1,0:T(8,128)(2,1)}, u32[]{:S(2)}) copy-start(bf16[1,1,1,5,128,128]{5,4,3,2,1,0:T(8,128)(2,1)} %param.12) | copy-start | bytes 491524
  31.8 8.4 %collective-permute-start.4 = (bf16[5,128,128]{2,1,0:T(8,128)(2,1)S(1)}, bf16[5,128,128]{2,1,0:T(8,128)(2,1)S(1)}, u32[]{:S(2)}, u32[]{:S(2)}) collective-permute-start(bf16[5,128,128]{2,1,0:T(8,128)(2,1)S(1)} %pack_joined.1), channel_id=1, source_target_pairs={{0,768},{128,384},{256,0},{384,640},{512,256},{640,896},{768,512},... | collective-permute-start | bytes 491528 | tf_op jit(solution)/shard_map/ppermute | solution.py:243

commit v5 on v4

--- a/solution.py
+++ b/solution.py
@@ -35,7 +35,9 @@
     return copies
 
 
-def pack_first_round(here_ref, parts_ref, far_ref, up_ref, down_ref, sems):
+def pack_first_round(
+    here_ref, parts_ref, far_ref, up_ref, down_ref, ahead_ref, behind_ref, own_ref, sems
+):
     size = parts_ref.shape[0]
     here = here_ref[0]
 
@@ -49,21 +51,9 @@
             (part(size - 3), down_ref.at[0]),
             (part(size - 1), down_ref.at[1]),
             (part(4), far_ref),
-        ],
-        sems,
-    )
-    for copy in copies:
-        copy.wait()
-
-
-def stage_own(here_ref, parts_ref, ahead_ref, behind_ref, own_ref, sems):
-    size = parts_ref.shape[0]
-    here = here_ref[0]
-    copies = fetch(
-        [
-            (parts_ref.at[lax.rem(here + 2, size)], ahead_ref),
-            (parts_ref.at[lax.rem(here + size - 2, size)], behind_ref),
-            (parts_ref.at[here], own_ref),
+            (part(2), ahead_ref),
+            (part(size - 2), behind_ref),
+            (part(0), own_ref),
         ],
         sems,
     )
@@ -136,7 +126,7 @@
         new_v_ref[b] = second.astype(new_v_ref.dtype)
 
 
-def flatten_rows(given_ref, rows_ref):
+def flatten_rows(given_ref, _, rows_ref):
     steps, width = given_ref.shape[1:]
     strip = 512
     for c in range(0, width, strip):
@@ -199,23 +189,14 @@
     pairs = jax.ShapeDtypeStruct((2,) + owned, parts.dtype)
     here = lax.axis_index("dp").reshape(1)
 
-    far, up, down = pl.pallas_call(
+    far, up, down, ahead, behind, own = pl.pallas_call(
         pack_first_round,
-        out_shape=(sums, pairs, pairs),
+        out_shape=(sums, pairs, pairs) + (pltpu.VMEM(owned, parts.dtype),) * 3,
         in_specs=[SMEM, ANY],
-        out_specs=(VMEM, VMEM, VMEM),
-        scratch_shapes=[pltpu.SemaphoreType.DMA((5,))],
+        out_specs=(VMEM,) * 6,
+        scratch_shapes=[pltpu.SemaphoreType.DMA((8,))],
         compiler_params=grant(4),
         name="pack_first_round",
-    )(here, parts)
-    ahead, behind, own = pl.pallas_call(
-        stage_own,
-        out_shape=[pltpu.VMEM(owned, parts.dtype)] * 3,
-        in_specs=[SMEM, ANY],
-        out_specs=[VMEM] * 3,
-        scratch_shapes=[pltpu.SemaphoreType.DMA((3,))],
-        compiler_params=grant(4),
-        name="stage_own",
     )(here, parts)
     opposite = [(i, (i - 2) % size if i % 2 == 0 else (i + 2) % size) for i in range(size)]
     far = lax.ppermute(far, "dp", opposite)
@@ -240,6 +221,7 @@
         compiler_params=grant(4),
         name="pack_joined",
     )(here, ahead, behind, up, down, far)
+    packed = joined
     joined = lax.ppermute(joined, "dp", opposite)
 
     near, chosen = pl.pallas_call(
@@ -277,11 +259,11 @@
     rows = pl.pallas_call(
         flatten_rows,
         out_shape=pltpu.VMEM((given.shape[0] * given.shape[1], model_width), given.dtype),
-        in_specs=[VMEM],
+        in_specs=[VMEM, ANY],
         out_specs=VMEM,
         compiler_params=grant(24),
         name="flatten_rows",
-    )(given)
+    )(given, packed)
     base = jnp.dot(rows, rollout_weight, preferred_element_type=jnp.float32)
     groups = 8
     decode_out, new_master, new_m, new_v, new_carry = pl.pallas_call(

time: 73.8 us -> 74 us (level)
  waiting for transfers between devices: 0.22 us -> 3.8 us
  local copies, waits for them, and re-layouts: 1.96 us -> 0.05 us
  Pallas kernels: 6.13 us -> 5.2 us
  starting transfers between devices: 31.9 us -> 31.1 us
    unnamed x14, local copies, waits for them, and re-layouts: 1.96 us -> 0.05 us
    ppermute x1, waiting for transfers between devices: 0.01 us -> 1.5 us  [on_device(): far = lax.ppermute(far, 'dp', opposite)]
    ppermute x1, waiting for transfers between devices: 0.01 us -> 1.21 us  [on_device(): up = lax.ppermute(up, 'dp', shifted(size, 1))]
    ppermute x1, starting transfers between devices: 3.09 us -> 1.92 us  [on_device(): plain = lax.ppermute(plain, 'dp', alike)]
    pallas_call x2 -> x1, Pallas kernels: 2.53 us -> 1.61 us  [on_device(): pl.pallas_call(pack_first_round, out_shape=(sums, pairs, pairs) + (pltpu....]
    ppermute x1, waiting for transfers between devices: 0.01 us -> 0.88 us  [on_device(): down = lax.ppermute(down, 'dp', shifted(size, -1))]
  transfers between devices with their start and end apart: 5 -> 5, of which waited for: 1 -> 4; matrix products, arithmetic and copies ran while one was open for 1% -> 1% of each run, Pallas kernels for 3% -> 2%
where the time goes in v5:
time: 74 us; the launch traced here: 73.8 us
  starting transfers between devices  31.1 us (42%)
  blocking collectives  30.5 us (41%)
  Pallas kernels  5.2 us (7%)
  waiting for transfers between devices  3.8 us (5%)
  between operations  1.47 us (2%)
  matrix products  1.01 us (1%)
    all_gather x1, blocking collectives, on_device(): gathered = lax.all_gather(sent, 'fsdp', axis=0, tiled=True)  30.5 us
    ppermute x1, starting transfers between devices, on_device(): down = lax.ppermute(down, 'dp', shifted(size, -1))  14 us
    ppermute x1, starting transfers between devices, on_device(): joined = lax.ppermute(joined, 'dp', opposite)  6.22 us
    ppermute x1, starting transfers between devices, on_device(): up = lax.ppermute(up, 'dp', shifted(size, 1))  5.87 us
    ppermute x1, starting transfers between devices, on_device(): far = lax.ppermute(far, 'dp', opposite)  3.09 us
    pallas_call x1, Pallas kernels, on_device(): pl.pallas_call(functools.partial(add_delta_product, groups), out_shape=[j...  2.01 us
    ppermute x1, starting transfers between devices, on_device(): plain = lax.ppermute(plain, 'dp', alike)  1.92 us
    pallas_call x1, Pallas kernels, on_device(): pl.pallas_call(pack_first_round, out_shape=(sums, pairs, pairs) + (pltpu....  1.61 us
  transfers between devices with their start and end apart: 5, of which 4 were waited for; matrix products, arithmetic and copies ran while one was open for 1% of the time, Pallas kernels for 2%

profile of v5, /device:TPU:1, one launch (start us, length us, event | category | flops | bytes accessed | tf_op | source)
XLA Modules:
  0.0 73.8 jit_solution(10612746495530203463)
XLA Ops:
  0.6 0.0 copy-start
  0.7 0.0 copy-start.1
  0.7 1.6 %pack_first_round.1 = (bf16[5,128,128]{2,1,0:T(8,128)(2,1)S(1)}, bf16[2,5,128,128]{3,2,1,0:T(8,128)(2,1)S(1)}, bf16[2,5,128,128]{3,2,1,0:T(8,128)(2,1)S(1)}, bf1...) custom-call(s32[1]{0:T(128)} %bitcast.1.here_ref, ...), custom_call_target="tpu_custom_call" | custom-call | tf_op jit(solution)/shard_map/pack_first_round/pallas_call | solution.py:192
  2.3 5.9 %collective-permute-start = (bf16[2,5,128,128]{3,2,1,0:T(8,128)(2,1)S(1)}, bf16[2,5,128,128]{3,2,1,0:T(8,128)(2,1)S(1)}, u32[]{:S(2)}, u32[]{:S(2)}) collective-permute-start(bf16[2,5,128,128]{3,2,1,0:T(8,128)(2,1)S(1)} %get-tuple-element.25), channel_id=1, source_target_pairs={{0,128},{128,256},{256,384},{384,512},{512,640},{640,768},{768,896... | collective-permute-start | bytes 983048 | tf_op jit(solution)/shard_map/ppermute | solution.py:203
  8.2 14.0 %collective-permute-start.1 = (bf16[2,5,128,128]{3,2,1,0:T(8,128)(2,1)S(1)}, bf16[2,5,128,128]{3,2,1,0:T(8,128)(2,1)S(1)}, u32[]{:S(2)}, u32[]{:S(2)}) collective-permute-start(bf16[2,5,128,128]{3,2,1,0:T(8,128)(2,1)S(1)} %get-tuple-element.26), channel_id=1, source_target_pairs={{0,896},{128,0},{256,128},{384,256},{512,384},{640,512},{768,640},... | collective-permute-start | bytes 983048 | tf_op jit(solution)/shard_map/ppermute | solution.py:204
  22.2 3.1 %collective-permute-start.2 = (bf16[5,128,128]{2,1,0:T(8,128)(2,1)S(1)}, bf16[5,128,128]{2,1,0:T(8,128)(2,1)S(1)}, u32[]{:S(2)}, u32[]{:S(2)}) collective-permute-start(bf16[5,128,128]{2,1,0:T(8,128)(2,1)S(1)} %get-tuple-element.27), channel_id=1, source_target_pairs={{0,768},{128,384},{256,0},{384,640},{512,256},{640,896},{768,512},... | collective-permute-start | bytes 491528 | tf_op jit(solution)/shard_map/ppermute | solution.py:202
  26.0 1.2 %collective-permute-done.up_ref = bf16[2,5,128,128]{3,2,1,0:T(8,128)(2,1)S(1)} collective-permute-done((bf16[2,5,128,128]{3,2,1,0:T(8,128)(2,1)S(1)}, bf16[2,5,128,128]{3,2,1,0:T(8,128)(2,1)S(1)}, u32[]{:S(2)}, u32[]{:S(2)}) %collective-permute-start) | collective-permute-done | bytes 327712 | tf_op jit(solution)/shard_map/ppermute | solution.py:203
  27.2 0.9 %collective-permute-done.1.down_ref = bf16[2,5,128,128]{3,2,1,0:T(8,128)(2,1)S(1)} collective-permute-done((bf16[2,5,128,128]{3,2,1,0:T(8,128)(2,1)S(1)}, bf16[2,5,128,128]{3,2,1,0:T(8,128)(2,1)S(1)}, u32[]{:S(2)}, u32[]{:S(2)}) %collective-permute-start.1) | collective-permute-done | bytes 327712 | tf_op jit(solution)/shard_map/ppermute | solution.py:204
  28.0 0.1 pack_plain.1
  28.1 1.9 %collective-permute-start.3 = (bf16[5,128,128]{2,1,0:T(8,128)(2,1)S(1)}, bf16[5,128,128]{2,1,0:T(8,128)(2,1)S(1)}, u32[]{:S(2)}, u32[]{:S(2)}) collective-permute-start(bf16[5,128,128]{2,1,0:T(8,128)(2,1)S(1)} %pack_plain.1), channel_id=1, source_target_pairs={{0,256},{128,896},{256,512},{384,128},{512,768},{640,384},{768,0},... | collective-permute-start | bytes 491528 | tf_op jit(solution)/shard_map/ppermute | solution.py:215
  30.1 1.5 %collective-permute-done.2.far_ref = bf16[5,128,128]{2,1,0:T(8,128)(2,1)S(1)} collective-permute-done((bf16[5,128,128]{2,1,0:T(8,128)(2,1)S(1)}, bf16[5,128,128]{2,1,0:T(8,128)(2,1)S(1)}, u32[]{:S(2)}, u32[]{:S(2)}) %collective-permute-start.2) | collective-permute-done | bytes 163872 | tf_op jit(solution)/shard_map/ppermute | solution.py:202
  31.6 0.1 pack_joined.1._
  31.7 6.2 %collective-permute-start.4 = (bf16[5,128,128]{2,1,0:T(8,128)(2,1)S(1)}, bf16[5,128,128]{2,1,0:T(8,128)(2,1)S(1)}, u32[]{:S(2)}, u32[]{:S(2)}) collective-permute-start(bf16[5,128,128]{2,1,0:T(8,128)(2,1)S(1)} %pack_joined.1._), channel_id=1, source_target_pairs={{0,768},{128,384},{256,0},{384,640},{512,256},{640,896},{768,512},... | collective-permute-start | bytes 491528 | tf_op jit(solution)/shard_map/ppermute | solution.py:225
  37.9 0.0 copy-done.1
  37.9 0.4 flatten_rows.1.rows
  38.3 0.0 copy-done
  38.3 0.0 copy-start.6
  38.3 0.0 copy-start.2
  38.3 0.0 copy-start.3
  38.3 0.0 copy-start.4
  38.4 0.0 copy-start.5
  38.4 1.0 %fusion.base_ref = f32[320,256]{1,0:T(8,128)S(1)} fusion(bf16[320,5120]{1,0:T(8,128)(2,1)S(1)} %flatten_rows.1.rows, bf16[5120,256]{1,0:T(8,128)(2,1)S(1)} %copy-done), kind=kOutput, calls=%fused_computation.1 | convolution fusion | flops 838860800 | bytes 6225920 | tf_op jit(solution)/shard_map/dot_general | solution.py:267
  39.4 0.0 copy-done.6
  39.4 0.6 sum_near.1
  40.0 0.0 collective-permute-done.3.plain_ref
  40.0 0.2 collective-permute-done.4.joined_ref
  40.2 0.0 copy-done.2
  40.2 0.0 copy-done.3
  40.2 0.0 copy-done.4
  40.2 0.0 copy-done.5
  40.2 0.4 adam_and_select.1
  40.7 30.5 %all-gather.1 = f16[80,128,128]{2,1,0:T(8,128)(2,1)S(1)} all-gather(f16[5,128,128]{2,1,0:T(8,128)(2,1)S(1)} %multiply_convert_fusion), channel_id=1, replica_groups=mesh['dp'=8,'fsdp'=16,'tensor'=8] {'fsdp'}, dimensions={0}, use_global_device_ids=true | all-gather | bytes 2785280 | tf_op jit(solution)/shard_map/all_gather | solution.py:254
  71.2 0.6 convert_element_type.11.blocks_ref
  71.8 2.0 %add_delta_product.1 = (bf16[80,4,256]{2,1,0:T(4,128)(2,1)}, f32[5,128,128]{2,1,0:T(8,128)}, bf16[5,128,128]{2,1,0:T(8,128)(2,1)}, bf16[5,128,128]{2,1,0:T(8,128)(2,1)}, f32[5,128,128]{2,1,0:T(8,128)}) custom-call(bf16[320,5120]{1,0:T(8,128)(2,1)S(1)} %flatten_rows.1.rows, bf16[80,128,128]{2,1,0:T(8,128)(2,1)S(1)} %convert_element_type.11.blocks_ref, ...), custom_call_target="tpu_custom_call" | custom-call | tf_op jit(solution)/shard_map/add_delta_product/pallas_call | solution.py:269
  (1 shorter events, 0.0 us)
Async XLA Ops:
  0.6 37.7 %copy-start = (bf16[5120,256]{1,0:T(8,128)(2,1)S(1)}, bf16[5120,256]{1,0:T(8,128)(2,1)}, u32[]{:S(2)}) copy-start(bf16[5120,256]{1,0:T(8,128)(2,1)} %param.16) | copy-start | bytes 7864324
  0.7 37.2 %copy-start.1 = (bf16[1,80,4,5120]{3,2,1,0:T(4,128)(2,1)S(1)}, bf16[1,80,4,5120]{3,2,1,0:T(4,128)(2,1)}, u32[]{:S(2)}) copy-start(bf16[1,80,4,5120]{3,2,1,0:T(4,128)(2,1)} %param.17) | copy-start | bytes 9830404
  2.3 24.9 %collective-permute-start = (bf16[2,5,128,128]{3,2,1,0:T(8,128)(2,1)S(1)}, bf16[2,5,128,128]{3,2,1,0:T(8,128)(2,1)S(1)}, u32[]{:S(2)}, u32[]{:S(2)}) collective-permute-start(bf16[2,5,128,128]{3,2,1,0:T(8,128)(2,1)S(1)} %get-tuple-element.25), channel_id=1, source_target_pairs={{0,128},{128,256},{256,384},{384,512},{512,640},{640,768},{768,896... | collective-permute-start | bytes 983048 | tf_op jit(solution)/shard_map/ppermute | solution.py:203
  8.2 19.9 %collective-permute-start.1 = (bf16[2,5,128,128]{3,2,1,0:T(8,128)(2,1)S(1)}, bf16[2,5,128,128]{3,2,1,0:T(8,128)(2,1)S(1)}, u32[]{:S(2)}, u32[]{:S(2)}) collective-permute-start(bf16[2,5,128,128]{3,2,1,0:T(8,128)(2,1)S(1)} %get-tuple-element.26), channel_id=1, source_target_pairs={{0,896},{128,0},{256,128},{384,256},{512,384},{640,512},{768,640},... | collective-permute-start | bytes 983048 | tf_op jit(solution)/shard_map/ppermute | solution.py:204
  22.2 9.3 %collective-permute-start.2 = (bf16[5,128,128]{2,1,0:T(8,128)(2,1)S(1)}, bf16[5,128,128]{2,1,0:T(8,128)(2,1)S(1)}, u32[]{:S(2)}, u32[]{:S(2)}) collective-permute-start(bf16[5,128,128]{2,1,0:T(8,128)(2,1)S(1)} %get-tuple-element.27), channel_id=1, source_target_pairs={{0,768},{128,384},{256,0},{384,640},{512,256},{640,896},{768,512},... | collective-permute-start | bytes 491528 | tf_op jit(solution)/shard_map/ppermute | solution.py:202
  28.1 11.9 %collective-permute-start.3 = (bf16[5,128,128]{2,1,0:T(8,128)(2,1)S(1)}, bf16[5,128,128]{2,1,0:T(8,128)(2,1)S(1)}, u32[]{:S(2)}, u32[]{:S(2)}) collective-permute-start(bf16[5,128,128]{2,1,0:T(8,128)(2,1)S(1)} %pack_plain.1), channel_id=1, source_target_pairs={{0,256},{128,896},{256,512},{384,128},{512,768},{640,384},{768,0},... | collective-permute-start | bytes 491528 | tf_op jit(solution)/shard_map/ppermute | solution.py:215
  31.7 8.6 %collective-permute-start.4 = (bf16[5,128,128]{2,1,0:T(8,128)(2,1)S(1)}, bf16[5,128,128]{2,1,0:T(8,128)(2,1)S(1)}, u32[]{:S(2)}, u32[]{:S(2)}) collective-permute-start(bf16[5,128,128]{2,1,0:T(8,128)(2,1)S(1)} %pack_joined.1._), channel_id=1, source_target_pairs={{0,768},{128,384},{256,0},{384,640},{512,256},{640,896},{768,512},... | collective-permute-start | bytes 491528 | tf_op jit(solution)/shard_map/ppermute | solution.py:225
  38.3 1.1 %copy-start.6 = (s32[1,1,1,5]{3,2,1,0:T(1,128)S(1)}, s32[1,1,1,5]{3,2,1,0:T(1,128)}, u32[]{:S(2)}) copy-start(s32[1,1,1,5]{3,2,1,0:T(1,128)} %param.15) | copy-start | bytes 64
  38.3 1.9 %copy-start.2 = (f32[1,1,1,5,128,128]{5,4,3,2,1,0:T(8,128)S(1)}, f32[1,1,1,5,128,128]{5,4,3,2,1,0:T(8,128)}, u32[]{:S(2)}) copy-start(f32[1,1,1,5,128,128]{5,4,3,2,1,0:T(8,128)} %param.10) | copy-start | bytes 983044
  38.3 1.9 %copy-start.3 = (f32[1,1,1,5,128,128]{5,4,3,2,1,0:T(8,128)S(1)}, f32[1,1,1,5,128,128]{5,4,3,2,1,0:T(8,128)}, u32[]{:S(2)}) copy-start(f32[1,1,1,5,128,128]{5,4,3,2,1,0:T(8,128)} %param.13) | copy-start | bytes 983044
  38.3 1.9 %copy-start.4 = (bf16[1,1,1,5,128,128]{5,4,3,2,1,0:T(8,128)(2,1)S(1)}, bf16[1,1,1,5,128,128]{5,4,3,2,1,0:T(8,128)(2,1)}, u32[]{:S(2)}) copy-start(bf16[1,1,1,5,128,128]{5,4,3,2,1,0:T(8,128)(2,1)} %param.11) | copy-start | bytes 491524
  38.4 1.9 %copy-start.5 = (bf16[1,1,1,5,128,128]{5,4,3,2,1,0:T(8,128)(2,1)S(1)}, bf16[1,1,1,5,128,128]{5,4,3,2,1,0:T(8,128)(2,1)}, u32[]{:S(2)}) copy-start(bf16[1,1,1,5,128,128]{5,4,3,2,1,0:T(8,128)(2,1)} %param.12) | copy-start | bytes 491524
